TPU v7x, 32 devices: a whole 2x2x4 slice. The times are simulated.
32 devices in a mesh: head: 4 (over y, core), expert: 8 (over z, x).
Axes of the slice: x: 2, y: 2, z: 4, core: 2. Of those that a mesh axis runs over, the one named last changes fastest.
Arguments:
- attention: bfloat16 [1024, 6144], P('expert', 'head'), may hold values from -6 to 6
- out_proj: bfloat16 [6144, 6144], P('head', 'expert'), may hold values from -0.078125 to 0.078125
- residual: bfloat16 [1024, 6144], P('expert', 'head'), may hold values from -64 to 64
- norm_gain: bfloat16 [6144], P('head'), may hold values from 0.25 to 1.75
- router: float32 [6144, 4], P('head'), may hold values from -0.02734375 to 0.02734375
- routes: int32 [1024, 2], P('expert'), may hold values from 0 to 3, all different within a row; in each aligned block of 128 rows (0 to 127, 128 to 255, ...) at most 72 rows name the same one
- cotangent: bfloat16 [1024, 6144], P('expert', 'head'), may hold values from -4 to 4
- gate_weight: bfloat16 [8, 6144, 4096], P('expert', None, 'head'), may hold values from -0.078125 to 0.078125
- up_weight: bfloat16 [8, 6144, 4096], P('expert', None, 'head'), may hold values from -0.078125 to 0.078125
- down_weight: bfloat16 [8, 4096, 6144], P('expert', None, 'head'), may hold values from -0.0625 to 0.0625
Outputs:
- layer_out: float32 [1024, 6144], P('expert', 'head')
- grad_gate: bfloat16 [8, 6144, 4096], P('expert', None, 'head')
- grad_up: bfloat16 [8, 6144, 4096], P('expert', None, 'head')
- grad_down: bfloat16 [8, 4096, 6144], P('expert', None, 'head')
Inputs may be any that keep to these rules, and one draw needn't show every extreme that they name: `routes`: each row names two different experts. In each aligned block of 128 rows (the rows of one index of expert) no expert is named by more than 72 rows, and in some block one expert is named by exactly 72 rows.
All inputs are finite; a program needn't handle non-finite values.
Results may differ from a plain program's by a relative error of at most 0.025.
Values may be sent and summed in bfloat16 or wider, within the bound.
No kernel may reach another device: no remote copies, remote signals or barrier semaphores. Data moves between devices by JAX's collectives and lax.ppermute only.
A program may use at most 192 MiB of HBM per device.

v0:
```python
import jax
import jax.numpy as jnp
from jax import lax
from jax.sharding import PartitionSpec as P

EPSILON = 1e-05


def shards(
    attention,
    out_proj,
    residual,
    norm_gain,
    router,
    routes,
    cotangent,
    gate_weight,
    up_weight,
    down_weight,
):
    heads_count = lax.axis_size("head")
    owners = lax.axis_size("expert")
    tok_rows = attention.shape[0]
    experts_count = router.shape[1]
    group_size = owners // experts_count
    width = residual.shape[1] * heads_count
    capacity = tok_rows * 9 // 16
    contract_rows = (((0,), (0,)), ((), ()))
    partial_value = jnp.dot(
        attention,
        lax.all_gather(out_proj, "expert", axis=1, tiled=True),
        preferred_element_type=jnp.float32,
    )
    proj = lax.psum_scatter(
        partial_value.astype(jnp.bfloat16), "head", scatter_dimension=1, tiled=True
    ).astype(jnp.float32)
    state = residual.astype(jnp.float32) + proj
    scaled = state * norm_gain.astype(jnp.float32)
    square_sum = jnp.sum(state * state, axis=1)
    raw_logits = jnp.dot(
        scaled, router, precision=lax.Precision.HIGHEST, preferred_element_type=jnp.float32
    )
    total_square, logit_sum = lax.psum((square_sum, raw_logits), "head")
    inverse = lax.rsqrt(total_square / width + EPSILON)[:, None]
    normed = (scaled * inverse).astype(jnp.bfloat16)
    logits = inverse * logit_sum
    expert_ids = jnp.arange(experts_count, dtype=jnp.int32)
    first_id = routes[:, 0]
    second = routes[:, 1]
    logit_first = jnp.sum(
        jnp.where(first_id[:, None] == expert_ids[None, :], logits, 0.0), axis=1, keepdims=True
    )
    logit_second = jnp.sum(
        jnp.where(second[:, None] == expert_ids[None, :], logits, 0.0), axis=1, keepdims=True
    )
    prob_first = jax.nn.sigmoid(logit_first - logit_second)
    prob_second = jax.nn.sigmoid(logit_second - logit_first)
    flat_routes = routes.reshape(-1)
    hit_table = (flat_routes[:, None] == expert_ids[None, :]).astype(jnp.int32)
    earlier = jnp.cumsum(hit_table, axis=0, dtype=jnp.int32) - hit_table
    slot_pair = jnp.sum(earlier * hit_table, axis=1, dtype=jnp.int32).reshape(tok_rows, 2)
    buffer_rows = experts_count * capacity
    row_ids = jnp.arange(buffer_rows, dtype=jnp.int32)
    row_expert = row_ids // capacity
    row_slot = row_ids % capacity
    place_first = (
        (first_id[None, :] == row_expert[:, None]) & (slot_pair[:, 0][None, :] == row_slot[:, None])
    ).astype(jnp.bfloat16)
    place_second = (
        (second[None, :] == row_expert[:, None]) & (slot_pair[:, 1][None, :] == row_slot[:, None])
    ).astype(jnp.bfloat16)
    place_either = place_first + place_second
    features = lax.all_gather(normed, "head", axis=1, tiled=True)
    send_rows = jnp.dot(place_either, features, preferred_element_type=jnp.float32).astype(
        jnp.bfloat16
    )
    send_rows = send_rows.reshape(experts_count, capacity, features.shape[1])
    cot_first = (prob_first * cotangent.astype(jnp.float32)).astype(jnp.bfloat16)
    cot_second = (prob_second * cotangent.astype(jnp.float32)).astype(jnp.bfloat16)
    send_cot = jnp.dot(place_first, cot_first, preferred_element_type=jnp.float32) + jnp.dot(
        place_second, cot_second, preferred_element_type=jnp.float32
    )
    send_cot = send_cot.astype(jnp.bfloat16).reshape(experts_count, capacity, cotangent.shape[1])
    copies_rows = jnp.repeat(send_rows, group_size, axis=0)
    copies_cot = jnp.repeat(send_cot, group_size, axis=0)
    got_rows, got_cot = (
        lax.all_to_all(copies_rows, "expert", split_axis=0, concat_axis=0, tiled=True),
        lax.all_to_all(copies_cot, "expert", split_axis=0, concat_axis=0, tiled=True),
    )
    rows_total = owners * capacity
    x_rows = got_rows.reshape(rows_total, width)
    cot_rows = got_cot.reshape(rows_total, cotangent.shape[1])
    gate_w = gate_weight[0]
    up_w = up_weight[0]
    down_w = down_weight[0]
    gate_val = lax.dot_general(
        gate_w, x_rows, (((0,), (1,)), ((), ())), preferred_element_type=jnp.float32
    )
    up_val = lax.dot_general(
        up_w, x_rows, (((0,), (1,)), ((), ())), preferred_element_type=jnp.float32
    )
    act_gate = jax.nn.silu(gate_val)
    hidden_local = (act_gate * up_val).astype(jnp.bfloat16)
    hidden_all = lax.all_gather(hidden_local, "head", axis=0, tiled=True)
    partial_out = lax.dot_general(
        hidden_all, down_w, contract_rows, preferred_element_type=jnp.float32
    )
    partial_out = partial_out.reshape(owners, capacity, down_w.shape[1])
    returned = lax.all_to_all(
        partial_out.astype(jnp.bfloat16), "expert", split_axis=0, concat_axis=0, tiled=True
    ).astype(partial_out.dtype)
    slot_out = jnp.sum(
        returned.reshape(experts_count, group_size, capacity, down_w.shape[1]), axis=1
    )
    slot_out = slot_out.astype(jnp.bfloat16).reshape(buffer_rows, down_w.shape[1])
    took_first = lax.dot_general(
        place_first, slot_out, contract_rows, preferred_element_type=jnp.float32
    )
    took_second = lax.dot_general(
        place_second, slot_out, contract_rows, preferred_element_type=jnp.float32
    )
    layer_out = state + prob_first * took_first + prob_second * took_second
    grad_down = jnp.dot(hidden_all, cot_rows, preferred_element_type=jnp.float32).astype(
        jnp.bfloat16
    )
    hidden_grad = lax.psum_scatter(
        lax.dot_general(
            down_w, cot_rows, (((1,), (1,)), ((), ())), preferred_element_type=jnp.float32
        ).astype(jnp.bfloat16),
        "head",
        scatter_dimension=0,
        tiled=True,
    ).astype(jnp.float32)
    gate_sigmoid = jax.nn.sigmoid(gate_val)
    gate_grad = (
        hidden_grad * up_val * gate_sigmoid * (1.0 + gate_val * (1.0 - gate_sigmoid))
    ).astype(jnp.bfloat16)
    up_grad = (hidden_grad * act_gate).astype(jnp.bfloat16)
    grad_gate = lax.dot_general(
        x_rows, gate_grad, (((0,), (1,)), ((), ())), preferred_element_type=jnp.float32
    ).astype(jnp.bfloat16)
    grad_up = lax.dot_general(
        x_rows, up_grad, (((0,), (1,)), ((), ())), preferred_element_type=jnp.float32
    ).astype(jnp.bfloat16)
    return (layer_out, grad_gate[None], grad_up[None], grad_down[None])


def solution(mesh):
    return jax.shard_map(
        shards,
        mesh=mesh,
        in_specs=(
            P("expert", "head"),
            P("head", "expert"),
            P("expert", "head"),
            P("head"),
            P("head", None),
            P("expert", None),
            P("expert", "head"),
            P("expert", None, "head"),
            P("expert", None, "head"),
            P("expert", None, "head"),
        ),
        out_specs=(
            P("expert", "head"),
            P("expert", None, "head"),
            P("expert", None, "head"),
            P("expert", None, "head"),
        ),
        check_vma=False,
    )
```

profile of v0, /device:TPU:0, one launch (start us, length us, event | category | flops | bytes accessed | tf_op | source)
XLA Modules:
  0.0 768.3 jit_solution(16970369013038629050)
XLA Ops:
  7.2 0.7 all-gather.4.cloned.1.call-update
  8.0 366.8 %all-gather.4.cloned.1.call-done = bf16[1536,6144]{1,0:T(8,128)(2,1)} async-done(((bf16[1536,768]{1,0:T(8,128)(2,1)}), bf16[1536,6144]{1,0:T(8,128)(2,1)}) %all-gather.4.cloned.1.call-update) | async-done | bytes 18874384 | tf_op jit(solution)/shard_map/all_gather | solution.py:31
  374.8 10.1 %convolution_convert_fusion.2 = bf16[128,6144]{1,0:T(8,128)(2,1)} fusion(bf16[128,1536]{1,0:T(8,128)(2,1)S(1)} %copy-done, bf16[1536,6144]{1,0:T(8,128)(2,1)} %all-gather.4.cloned.1.call-done), kind=kOutput, calls=%fused_computation.13 | convolution fusion | flops 2416705536 | bytes 20840448 | tf_op jit(solution)/shard_map/dot_general | solution.py:29
  385.3 1.2 reduce-window.6
  387.3 25.9 %reduce-scatter.3.cloned.1.call-done = bf16[128,1536]{1,0:T(8,128)(2,1)} async-done(((bf16[128,6144]{1,0:T(8,128)(2,1)}), bf16[128,1536]{1,0:T(8,128)(2,1)}) %reduce-scatter.3.cloned.1.call-update) | async-done | bytes 393232 | tf_op jit(solution)/shard_map/reduce_scatter | solution.py:34
  413.2 1.2 multiply_reduce_fusion
  414.4 1.8 fusion.35
  416.2 5.7 all-reduce
  422.0 0.5 fusion.38
  422.5 0.5 fusion.18
  423.0 1.3 broadcast_in_dim.17
  424.3 5.8 all-to-all-start.2
  430.2 0.9 multiply_convert_fusion
  431.1 23.1 %all-gather.6.cloned.1.call-done = bf16[128,6144]{1,0:T(8,128)(2,1)} async-done(((bf16[128,1536]{1,0:T(8,128)(2,1)}), bf16[128,6144]{1,0:T(8,128)(2,1)}) %all-gather.6.cloned.1.call-update) | async-done | bytes 1572880 | tf_op jit(solution)/shard_map/all_gather | solution.py:73
  454.2 4.3 convolution_convert_fusion.1
  458.6 12.5 %all-to-all-done.2 = bf16[8,72,1536]{2,1,0:T(8,128)(2,1)S(1)} async-done(((bf16[8,72,1536]{2,1,0:T(8,128)(2,1)}), bf16[8,72,1536]{2,1,0:T(8,128)(2,1)S(1)}, u32[]{:S(2)}, u32[]{:S(2)}) %all-to-all-start.2) | async-done | bytes 1769504 | tf_op jit(solution)/shard_map/all_to_all | solution.py:88
  471.1 6.5 broadcast_in_dim.16
  477.6 4.8 all-to-all-start
  482.5 18.4 %fusion.12 = bf16[4096,576]{0,1:T(8,128)(2,1)} fusion(bf16[576,1536]{1,0:T(8,128)(2,1)S(1)} %bitcast.112, bf16[1,4096,1536]{2,1,0:T(8,128)(2,1)} %param.19), kind=kOutput, calls=%fused_computation.15 | convolution fusion | flops 7250116608 | bytes 19070976 | tf_op jit(solution)/shard_map/dot_general | solution.py:127
  501.1 135.4 %all-to-all-done = bf16[8,72,6144]{2,1,0:T(8,128)(2,1)} async-done(((bf16[8,72,6144]{2,1,0:T(8,128)(2,1)}), bf16[8,72,6144]{2,1,0:T(8,128)(2,1)}, u32[]{:S(2)}, u32[]{:S(2)}) %all-to-all-start) | async-done | bytes 7077920 | tf_op jit(solution)/shard_map/all_to_all | solution.py:87
  636.5 12.5 %fusion.7 = f32[576,1024]{1,0:T(8,128)S(1)} fusion(bf16[576,6144]{1,0:T(8,128)(2,1)} %bitcast.6, bf16[1,6144,1024]{2,1,0:T(8,128)(2,1)} %param.17), kind=kOutput, calls=%fused_computation.8 | convolution fusion | flops 7247757312 | bytes 22020096 | tf_op jit(solution)/shard_map/dot_general | solution.py:96
  649.0 14.7 %fusion.25 = (bf16[1024,576]{0,1:T(8,128)(2,1)}, f32[576,1024]{1,0:T(8,128)}) fusion(f32[576,1024]{1,0:T(8,128)S(1)} %fusion.7, bf16[576,6144]{1,0:T(8,128)(2,1)} %bitcast.6, bf16[1,6144,1024]{2,1,0:T(8,128)(2,1)} %param.18), kind=kOutput, calls=%fused_computation.30 | convolution fusion | flops 7251296256 | bytes 25559040 | tf_op jit(solution)/shard_map/dot_general | solution.py:99
  663.7 17.1 %convert_bitcast_fusion.1 = bf16[1,6144,1024]{2,1,0:T(8,128)(2,1)} fusion(bf16[576,6144]{1,0:T(8,128)(2,1)} %bitcast.6, bf16[1024,576]{0,1:T(8,128)(2,1)} %reduce-scatter.5.cloned.1.call-done, f32[576,1024]{1,0:T(8,128)} %get-tuple-element.15, f32[576,1024]{1,0:T(8,128)} %copy-done.10), kind=kOutput, calls=%fused_computation.11 | convolution fusion | flops 7260536832 | bytes 25559040 | tf_op jit(solution)/shard_map/dot_general | solution.py:139
  680.8 18.6 %all-gather.8.cloned.1.call-done = bf16[4096,576]{0,1:T(8,128)(2,1)} async-done(((bf16[1024,576]{0,1:T(8,128)(2,1)}), bf16[4096,576]{0,1:T(8,128)(2,1)}) %all-gather.8.cloned.1.call-update) | async-done | bytes 4718608 | tf_op jit(solution)/shard_map/all_gather | solution.py:104
  699.4 12.9 %fusion.15 = bf16[8,72,1536]{2,1,0:T(8,128)(2,1)} fusion(bf16[8,72,4096]{2,1,0:T(8,128)(2,1)} %bitcast.115, bf16[1,4096,1536]{2,1,0:T(8,128)(2,1)} %param.19), kind=kOutput, calls=%fused_computation.16 | convolution fusion | flops 7248642048 | bytes 19070976 | tf_op jit(solution)/shard_map/dot_general | solution.py:105
  712.3 5.5 all-to-all-start.1
  717.8 16.4 %convert_bitcast_fusion = bf16[1,6144,1024]{2,1,0:T(8,128)(2,1)} fusion(bf16[576,6144]{1,0:T(8,128)(2,1)} %bitcast.6, bf16[1024,576]{0,1:T(8,128)(2,1)} %reduce-scatter.5.cloned.1.call-done, f32[576,1024]{1,0:T(8,128)} %copy-done.10), kind=kOutput, calls=%fused_computation.10 | convolution fusion | flops 7258177536 | bytes 23199744 | tf_op jit(solution)/shard_map/dot_general | solution.py:142
  734.2 14.8 %fusion = bf16[1,4096,1536]{2,1,0:T(8,128)(2,1)} fusion(bf16[4096,576]{0,1:T(8,128)(2,1)} %all-gather.8.cloned.1.call-done, bf16[576,1536]{1,0:T(8,128)(2,1)S(1)} %bitcast.113), kind=kOutput, calls=%fused_computation.1 | convolution fusion | flops 7254048768 | bytes 19070976 | tf_op jit(solution)/shard_map/dot_general | solution.py:123
  749.0 10.4 %all-to-all-done.1 = bf16[8,72,1536]{2,1,0:T(8,128)(2,1)S(1)} async-done(((bf16[8,72,1536]{2,1,0:T(8,128)(2,1)}), bf16[8,72,1536]{2,1,0:T(8,128)(2,1)S(1)}, u32[]{:S(2)}, u32[]{:S(2)}) %all-to-all-start.1) | async-done | bytes 1769504 | tf_op jit(solution)/shard_map/all_to_all | solution.py:109
  759.5 0.3 bitcast_reduce_fusion
  759.8 0.6 fusion.20
  760.4 1.4 fusion.19
  (51 shorter events, 1.7 us)
Async XLA Ops:
  7.2 367.6 %copy-start = (bf16[128,1536]{1,0:T(8,128)(2,1)S(1)}, bf16[128,1536]{1,0:T(8,128)(2,1)}, u32[]{:S(2)}) copy-start(bf16[128,1536]{1,0:T(8,128)(2,1)} %param.10) | copy-start | bytes 1179652
  7.2 367.6 %all-gather.4.cloned.1.call-start = ((), (), s32[]{:S(2)}) async-start(), calls=%async_computation.5 | async-start | bytes 21233664 | tf_op jit(solution)/shard_map/all_gather | solution.py:31
  7.9 377.0 %copy-start.8 = (s32[128,2]{0,1:T(2,128)S(1)}, s32[128,2]{0,1:T(2,128)}, u32[]{:S(2)}) copy-start(s32[128,2]{0,1:T(2,128)} %param.15) | copy-start | bytes 3076
  7.9 377.4 %copy-start.9 = (bf16[1536]{0:T(1024)(128)(2,1)S(1)}, bf16[1536]{0:T(1024)(128)(2,1)}, u32[]{:S(2)}) copy-start(bf16[1536]{0:T(1024)(128)(2,1)} %param.13) | copy-start | bytes 9220
  7.9 405.3 %copy-start.2 = (bf16[128,1536]{1,0:T(8,128)(2,1)S(1)}, bf16[128,1536]{1,0:T(8,128)(2,1)}, u32[]{:S(2)}) copy-start(bf16[128,1536]{1,0:T(8,128)(2,1)} %param.12) | copy-start | bytes 1179652
  7.9 405.3 %reduce-scatter.3.cloned.1.call-start = ((), (), s32[]{:S(2)}) async-start(), calls=%async_computation.6 | async-start | bytes 1966080 | tf_op jit(solution)/shard_map/reduce_scatter | solution.py:34
  384.9 29.5 %copy-start.7 = (f32[1536,4]{0,1:T(4,128)S(1)}, f32[1536,4]{0,1:T(4,128)}, u32[]{:S(2)}) copy-start(f32[1536,4]{0,1:T(4,128)} %param.14) | copy-start | bytes 73732
  384.9 37.1 %copy-start.6 = (bf16[128,1536]{1,0:T(8,128)(2,1)S(1)}, bf16[128,1536]{1,0:T(8,128)(2,1)}, u32[]{:S(2)}) copy-start(bf16[128,1536]{1,0:T(8,128)(2,1)} %param.16) | copy-start | bytes 1179652
  424.3 5.9 copy-start.3
  424.3 46.8 %all-to-all-start.2 = ((bf16[8,72,1536]{2,1,0:T(8,128)(2,1)}), bf16[8,72,1536]{2,1,0:T(8,128)(2,1)S(1)}, u32[]{:S(2)}, u32[]{:S(2)}) async-start(bf16[8,72,1536]{2,1,0:T(8,128)(2,1)} %bitcast.18), calls=%async_computation.3 | async-start | bytes 3538944 | tf_op jit(solution)/shard_map/all_to_all | solution.py:88
  430.2 24.1 %all-gather.6.cloned.1.call-start = ((), (), s32[]{:S(2)}) async-start(), calls=%async_computation.7 | async-start | bytes 1966080 | tf_op jit(solution)/shard_map/all_gather | solution.py:73
  471.1 11.4 %copy-start.4 = (bf16[8,72,1536]{2,1,0:T(8,128)(2,1)}, bf16[8,72,1536]{2,1,0:T(8,128)(2,1)S(1)}, u32[]{:S(2)}) copy-start(bf16[8,72,1536]{2,1,0:T(8,128)(2,1)S(1)} %all-to-all-done.2) | copy-start | bytes 5308420
  477.6 158.9 %all-to-all-start = ((bf16[8,72,6144]{2,1,0:T(8,128)(2,1)}), bf16[8,72,6144]{2,1,0:T(8,128)(2,1)}, u32[]{:S(2)}, u32[]{:S(2)}) async-start(bf16[8,72,6144]{2,1,0:T(8,128)(2,1)} %bitcast.107), calls=%async_computation.1 | async-start | bytes 14155776 | tf_op jit(solution)/shard_map/all_to_all | solution.py:87
  482.4 181.3 %reduce-scatter.5.cloned.1.call-start = ((), (), s32[]{:S(2)}) async-start(), calls=%async_computation.9 | async-start | bytes 5898240 | tf_op jit(solution)/shard_map/reduce_scatter | solution.py:126
  500.9 198.5 %all-gather.8.cloned.1.call-start = ((), (), s32[]{:S(2)}) async-start(), calls=%async_computation.8 | async-start | bytes 5898240 | tf_op jit(solution)/shard_map/all_gather | solution.py:104
  648.9 14.7 %copy-start.10 = (f32[576,1024]{1,0:T(8,128)}, f32[576,1024]{1,0:T(8,128)S(1)}, u32[]{:S(2)}) copy-start(f32[576,1024]{1,0:T(8,128)S(1)} %fusion.7) | copy-start | bytes 7077892
  712.3 47.1 %all-to-all-start.1 = ((bf16[8,72,1536]{2,1,0:T(8,128)(2,1)}), bf16[8,72,1536]{2,1,0:T(8,128)(2,1)S(1)}, u32[]{:S(2)}, u32[]{:S(2)}) async-start(bf16[8,72,1536]{2,1,0:T(8,128)(2,1)} %fusion.15), calls=%async_computation.2 | async-start | bytes 3538944 | tf_op jit(solution)/shard_map/all_to_all | solution.py:109
  717.8 16.4 %copy-start.5 = (bf16[8,72,1536]{2,1,0:T(8,128)(2,1)S(1)}, bf16[8,72,1536]{2,1,0:T(8,128)(2,1)}, u32[]{:S(2)}) copy-start(bf16[8,72,1536]{2,1,0:T(8,128)(2,1)} %copy-done.4) | copy-start | bytes 5308420
  759.8 2.0 copy-start.1
Sparse Core Ops, SparseCore 0:
  9.6 365.1 all-gather.3
  385.0 28.1 reduce-scatter.2
  433.2 20.9 all-gather.5
  501.0 48.2 reduce-scatter.4
  663.8 35.5 all-gather.7
where the time goes:
time: 769 us; the launch traced here: 768 us
  waiting for transfers between devices  593 us (77%)
  matrix products  126 us (16%)
  starting transfers between devices  16.6 us (2%)
  between operations  14 us (2%)
  local copies, waits for them, and re-layouts  8.86 us (1%)
    all_gather x1, waiting for transfers between devices, shards(): lax.all_gather(out_proj, 'expert', axis=1, tiled=True)  367 us
    all_to_all x1, waiting for transfers between devices, shards(): lax.all_to_all(copies_rows, 'expert', split_axis=0, concat_axis=0, tiled=...  135 us
    reduce_scatter x1, waiting for transfers between devices, shards(): lax.psum_scatter(partial_value.astype(jnp.bfloat16), 'head', scatter_dime...  25.9 us
    all_gather x1, waiting for transfers between devices, shards(): features = lax.all_gather(normed, 'head', axis=1, tiled=True)  23.1 us
    all_gather x1, waiting for transfers between devices, shards(): hidden_all = lax.all_gather(hidden_local, 'head', axis=0, tiled=True)  18.6 us
    dot_general x1, matrix products, shards(): lax.dot_general(down_w, cot_rows, (((1,), (1,)), ((), ())), preferred_ele...  18.4 us
    dot_general x1, matrix products, shards(): lax.dot_general(x_rows, gate_grad, (((0,), (1,)), ((), ())), preferred_el...  17.1 us
    dot_general x1, matrix products, shards(): lax.dot_general(x_rows, up_grad, (((0,), (1,)), ((), ())), preferred_elem...  16.4 us
  transfers between devices with their start and end apart: 8, of which 7 were waited for; matrix products, arithmetic and copies ran while one was open for 13% of the time, Pallas kernels for 0%

commit v1 on v0

v1 whole, which is shorter than its diff:
```python
import functools

import jax
import jax.numpy as jnp
from jax import lax
from jax.experimental import pallas as pl
from jax.experimental.pallas import tpu as pltpu
from jax.sharding import Mesh, PartitionSpec as P

EPSILON = 1e-05
EXPERTS = 4
CORES = 2
LANES = 128
VMEM = 50 * 2**20
BF = jnp.bfloat16
F32 = jnp.float32
ALL_AXES = ("y", "c", "z", "x")


def shift(value, axis, step=1):
    size = lax.axis_size(axis)
    return lax.ppermute(value, axis, [(i, (i + step) % size) for i in range(size)])


def pick(stack, index, axis=0):
    return lax.dynamic_index_in_dim(stack, index, axis, keepdims=False)


def tie(*values):
    return lax.optimization_barrier(values)


def swap_pairs(n_y, n_z, n_x, parts, turn):
    pairs = []
    for y in range(n_y):
        for c in range(CORES):
            for z in range(n_z):
                for x in range(n_x):
                    piece = (y * CORES + c) * parts + (turn + z) % parts
                    to_z, to_c = piece // CORES, piece % CORES
                    to_y = z // parts
                    source = ((y * CORES + c) * n_z + z) * n_x + x
                    target = ((to_y * CORES + to_c) * n_z + to_z) * n_x + x
                    pairs.append((source, target))
    return pairs


def dot32(a, b, dims):
    return lax.dot_general(a, b, (dims, ((), ())), preferred_element_type=F32)


def sigmoid(value):
    return 1.0 / (1.0 + jnp.exp(-value))


def order(mine, other, index):
    first = index == 0
    return jnp.where(first, mine, other), jnp.where(first, other, mine)


def place_copies(plan, refs, scratch, sems):
    copies = []
    for number, (ref, lead, row, col) in enumerate(plan):
        source = refs[ref] if lead is None else refs[ref].at[lead]
        n_rows, n_cols = source.shape
        row = pl.multiple_of(row(), 16) if callable(row) else row
        col = pl.multiple_of(col(), LANES) if callable(col) else col
        copies.append(
            pltpu.make_async_copy(
                source,
                scratch.at[pl.ds(row, n_rows), pl.ds(col, n_cols)],
                sems.at[number],
            )
        )
    return copies


def whole(shape):
    return pl.BlockSpec(shape, lambda *_: (0,) * len(shape))


def column_tile(cols):
    return 256 if cols % 256 == 0 else cols


def params():
    return pltpu.CompilerParams(vmem_limit_bytes=VMEM)


def cost(flops, bytes_accessed, transcendentals=0):
    return pl.CostEstimate(
        flops=flops, bytes_accessed=bytes_accessed, transcendentals=transcendentals
    )


def forward_kernel(plan, n_refs, width, *args):
    refs = args[:n_refs]
    gate_w, up_w, stats, meta, hid, a_out, b_out, scale, x_out = args[n_refs:-5]
    x_all, inv, prob, sems, sem = args[-5:]
    step = pl.program_id(0)
    rows = x_all.shape[0]
    keep = pltpu.make_async_copy(x_all, x_out, sem)

    @pl.when(step == 0)
    def _():
        copies = place_copies(plan, refs, x_all, sems)
        for copy in copies:
            copy.start()
        for copy in copies:
            copy.wait()
        keep.start()
        raw = stats[...]
        mean = raw[:, LANES - 1 :] / width
        inv[...] = jnp.broadcast_to(lax.rsqrt(mean + EPSILON), (rows, LANES))
        lane = lax.broadcasted_iota(jnp.int32, (rows, LANES), 1)
        own = lax.axis_index("z")
        other = meta[...].astype(F32).astype(jnp.int32) - own
        expert = lane % EXPERTS
        sign = (expert == own).astype(F32) - (expert == other).astype(F32)
        sign = jnp.where(lane < 3 * EXPERTS, sign, 0.0)
        gap = jnp.sum(raw * sign, axis=1, keepdims=True) * inv[...]
        prob[...] = sigmoid(gap)
        scale[...] = prob[...] * inv[...]

    x = x_all[...]
    a = jnp.dot(x, gate_w[...], preferred_element_type=F32)
    b = jnp.dot(x, up_w[...], preferred_element_type=F32)
    inverse = inv[:, :1]
    a = a * inverse
    b = b * inverse
    hid[...] = (a * sigmoid(a) * b * prob[:, :1]).astype(BF)
    a_out[...] = a
    b_out[...] = b

    @pl.when(step == pl.num_programs(0) - 1)
    def _():
        keep.wait()


def forward(pieces, plan, gate_w, up_w, stats, meta, meta_block):
    width, cols = gate_w.shape
    rows = meta.shape[0]
    tile = 256 if cols % 256 == 0 else cols
    anywhere = pl.BlockSpec(memory_space=pl.ANY)
    return pl.pallas_call(
        functools.partial(forward_kernel, plan, len(pieces), width),
        grid=(cols // tile,),
        in_specs=[anywhere] * len(pieces)
        + [
            pl.BlockSpec((width, tile), lambda j: (0, j)),
            pl.BlockSpec((width, tile), lambda j: (0, j)),
            whole((rows, LANES)),
            pl.BlockSpec((rows, LANES), lambda j: (0, meta_block)),
        ],
        out_specs=[
            pl.BlockSpec((rows, tile), lambda j: (0, j)),
            pl.BlockSpec((rows, tile), lambda j: (0, j)),
            pl.BlockSpec((rows, tile), lambda j: (0, j)),
            whole((rows, LANES)),
            anywhere,
        ],
        out_shape=[
            jax.ShapeDtypeStruct((rows, cols), BF),
            jax.ShapeDtypeStruct((rows, cols), F32),
            jax.ShapeDtypeStruct((rows, cols), F32),
            jax.ShapeDtypeStruct((rows, LANES), F32),
            jax.ShapeDtypeStruct((rows, width), BF),
        ],
        scratch_shapes=[
            pltpu.VMEM((rows, width), BF),
            pltpu.VMEM((rows, LANES), F32),
            pltpu.VMEM((rows, LANES), F32),
            pltpu.SemaphoreType.DMA((len(plan),)),
            pltpu.SemaphoreType.DMA,
        ],
        compiler_params=pltpu.CompilerParams(vmem_limit_bytes=VMEM),
        cost_estimate=pl.CostEstimate(
            flops=4 * rows * width * cols,
            bytes_accessed=4 * width * cols + 2 * rows * width,
            transcendentals=rows * cols,
        ),
    )(*pieces, gate_w, up_w, stats, meta)


def gate_up_kernel(x, a_in, b_in, dh, scale, gate_out, up_out, da, db):
    @pl.when(pl.program_id(0) == 0)
    def _():
        cols = a_in.shape[1]
        for k in range(cols // LANES):
            at = slice(k * LANES, (k + 1) * LANES)
            a, b = a_in[:, at], b_in[:, at]
            s = sigmoid(a)
            grad = dh[:, at].astype(F32) * scale[...]
            da[:, at] = (grad * b * s * (1.0 + a * (1.0 - s))).astype(BF)
            db[:, at] = (grad * a * s).astype(BF)

    gate_out[...] = dot32(x[...], da[...], ((0,), (0,))).astype(BF)
    up_out[...] = dot32(x[...], db[...], ((0,), (0,))).astype(BF)


def gate_up_grads(x_rows, a, b, dh, scale):
    rows, width = x_rows.shape
    cols = a.shape[1]
    tile = 512
    out = pl.BlockSpec((tile, cols), lambda j: (j, 0))
    return pl.pallas_call(
        gate_up_kernel,
        grid=(width // tile,),
        in_specs=[
            pl.BlockSpec((rows, tile), lambda j: (0, j)),
            whole((rows, cols)),
            whole((rows, cols)),
            whole((rows, cols)),
            whole((rows, LANES)),
        ],
        out_specs=[out, out],
        out_shape=[jax.ShapeDtypeStruct((width, cols), BF)] * 2,
        scratch_shapes=[pltpu.VMEM((rows, cols), BF)] * 2,
        compiler_params=pltpu.CompilerParams(vmem_limit_bytes=VMEM),
        cost_estimate=pl.CostEstimate(
            flops=4 * rows * width * cols,
            bytes_accessed=4 * width * cols + 2 * rows * width + 10 * rows * cols,
            transcendentals=rows * cols,
        ),
    )(x_rows, a, b, dh, scale)


def down_store(value, out, split_rows):
    if split_rows is None:
        out[...] = value
        return
    n_y, n_x, size = split_rows
    for y in range(n_y):
        for x in range(n_x):
            at = (y * n_x + x) * size
            out[x, y * size : (y + 1) * size, :] = value[at : at + size]


def down_kernel(plan, n_refs, split_rows, *args):
    refs = args[:n_refs]
    down_w, out, hid_out, hid, sems, sem = args[n_refs:]
    step = pl.program_id(0)
    keep = pltpu.make_async_copy(hid, hid_out, sem)

    @pl.when(step == 0)
    def _():
        copies = place_copies(plan, refs, hid, sems)
        for copy in copies:
            copy.start()
        for copy in copies:
            copy.wait()
        keep.start()

    value = jnp.dot(hid[...], down_w[...], preferred_element_type=F32).astype(BF)
    down_store(value, out, split_rows)

    @pl.when(step == pl.num_programs(0) - 1)
    def _():
        keep.wait()


def down_next_kernel(split_rows, hid, down_w, out):
    value = jnp.dot(hid[...], down_w[...], preferred_element_type=F32).astype(BF)
    down_store(value, out, split_rows)


def down_specs(rows, hidden, tile, feats, base, split_rows):
    weight = pl.BlockSpec((hidden, tile), lambda j: (0, j + base))
    if split_rows is None:
        out = pl.BlockSpec((rows, tile), lambda j: (0, j))
        shape = jax.ShapeDtypeStruct((rows, feats), BF)
    else:
        n_y, n_x, size = split_rows
        out = pl.BlockSpec((n_x, n_y * size, tile), lambda j: (0, 0, j))
        shape = jax.ShapeDtypeStruct((n_x, n_y * size, feats), BF)
    return weight, out, shape


def down_first(pieces, plan, down_w, feats, rows, split_rows):
    hidden = down_w.shape[0]
    tile = column_tile(feats)
    anywhere = pl.BlockSpec(memory_space=pl.ANY)
    weight, out, shape = down_specs(rows, hidden, tile, feats, 0, split_rows)
    return pl.pallas_call(
        functools.partial(down_kernel, plan, len(pieces), split_rows),
        grid=(feats // tile,),
        in_specs=[anywhere] * len(pieces) + [weight],
        out_specs=[out, anywhere],
        out_shape=[shape, jax.ShapeDtypeStruct((rows, hidden), BF)],
        scratch_shapes=[
            pltpu.VMEM((rows, hidden), BF),
            pltpu.SemaphoreType.DMA((len(plan),)),
            pltpu.SemaphoreType.DMA,
        ],
        compiler_params=params(),
        cost_estimate=cost(
            2 * rows * hidden * feats, 2 * hidden * feats + 4 * rows * hidden
        ),
    )(*pieces, down_w)


def down_next(hidden_all, down_w, start, feats, split_rows):
    rows, hidden = hidden_all.shape
    tile = column_tile(feats)
    weight, out, shape = down_specs(rows, hidden, tile, feats, start // tile, split_rows)
    return pl.pallas_call(
        functools.partial(down_next_kernel, split_rows),
        grid=(feats // tile,),
        in_specs=[whole((rows, hidden)), weight],
        out_specs=out,
        out_shape=shape,
        compiler_params=params(),
        cost_estimate=cost(
            2 * rows * hidden * feats, 2 * hidden * feats + 2 * rows * hidden
        ),
    )(hidden_all, down_w)


def down_grad_kernel(hid, cot, out):
    out[...] = dot32(hid[...], cot[...], ((0,), (0,))).astype(BF)


def down_grad(hidden_all, cot_rows, feats):
    rows, hidden = hidden_all.shape
    tile = 512
    return pl.pallas_call(
        down_grad_kernel,
        grid=(hidden // tile,),
        in_specs=[
            pl.BlockSpec((rows, tile), lambda j: (0, j)),
            pl.BlockSpec((rows, feats), lambda j: (0, 0)),
        ],
        out_specs=pl.BlockSpec((tile, feats), lambda j: (j, 0)),
        out_shape=jax.ShapeDtypeStruct((hidden, feats), BF),
        compiler_params=pltpu.CompilerParams(vmem_limit_bytes=VMEM),
        cost_estimate=pl.CostEstimate(
            flops=2 * rows * hidden * feats,
            bytes_accessed=2 * hidden * feats + 2 * rows * hidden,
            transcendentals=0,
        ),
    )(hidden_all, cot_rows)


def row_stats_kernel(x, split, weight, out):
    n_z, rows, cols = x.shape
    total = jnp.zeros((rows, LANES), F32)
    raw = jnp.zeros((rows, LANES), F32)
    for z in range(n_z):
        raw = raw + dot32(x[z], split[z], ((1,), (1,)))
        for k in range(cols // LANES):
            at = slice(k * LANES, (k + 1) * LANES)
            part = x[z, :, at].astype(F32)
            total = total + part * part * weight[z, :, at]
    lane = lax.broadcasted_iota(jnp.int32, (rows, LANES), 1)
    out[...] = jnp.where(lane == LANES - 1, jnp.sum(total, axis=1, keepdims=True), raw)


def row_stats(x_got, split, weight):
    n_z, rows, cols = x_got.shape
    return pl.pallas_call(
        row_stats_kernel,
        out_shape=jax.ShapeDtypeStruct((rows, LANES), F32),
        compiler_params=pltpu.CompilerParams(vmem_limit_bytes=VMEM),
        cost_estimate=pl.CostEstimate(
            flops=2 * n_z * rows * cols * LANES,
            bytes_accessed=2 * n_z * cols * (rows + LANES),
            transcendentals=0,
        ),
    )(x_got, split, weight)


def hidden_grad_kernel(heads, cot, down_w, out):
    out[0] = dot32(cot[...], down_w[...], ((1,), (1,))).astype(BF)


def hidden_grad_part(heads, cot_rows, down_w, cols):
    rows, feats = cot_rows.shape[0], down_w.shape[1]
    tile = 512 if cols % 512 == 0 else cols
    steps = cols // tile
    n_heads = heads.shape[0]
    return pl.pallas_call(
        hidden_grad_kernel,
        grid_spec=pltpu.PrefetchScalarGridSpec(
            num_scalar_prefetch=1,
            grid=(n_heads, steps),
            in_specs=[
                pl.BlockSpec((rows, feats), lambda i, j, heads: (0, 0)),
                pl.BlockSpec((tile, feats), lambda i, j, heads: (heads[i] * steps + j, 0)),
            ],
            out_specs=pl.BlockSpec((1, rows, tile), lambda i, j, heads: (i, 0, j)),
        ),
        out_shape=jax.ShapeDtypeStruct((n_heads, rows, cols), BF),
        compiler_params=pltpu.CompilerParams(vmem_limit_bytes=VMEM),
        cost_estimate=pl.CostEstimate(
            flops=2 * rows * feats * cols * n_heads,
            bytes_accessed=2 * n_heads * cols * (feats + rows),
            transcendentals=0,
        ),
    )(heads, cot_rows, down_w)


def gather_plane(own):
    n_y, n_x, n_z = lax.axis_size("y"), lax.axis_size("x"), own.shape[0]
    rows, cols = own.shape[1:]
    if n_y != 2 or n_x != 2 or rows % 16:
        full = lax.all_gather(own, ("y", "x", "c"), axis=0, tiled=False)
        full = full.reshape(n_y, n_x, CORES, n_z, rows, cols).transpose(0, 1, 4, 3, 2, 5)
        full = full.reshape(n_y * n_x * rows, n_z * CORES * cols)
        return [full], [(0, None, 0, 0)], full
    half = n_z // 2
    side = shift(own, "x")
    over = shift(own, "y")
    corner_low = shift(over[:half], "x")
    corner_high = shift(side[half:], "y")
    found = [
        (own, 0, 0, 0),
        (side, 0, 1, 0),
        (over, 1, 0, 0),
        (corner_low, 1, 1, 0),
        (corner_high, 1, 1, half),
    ]
    pieces, plan = [], []
    for value, dy, dx, low in found:
        for dc, array in enumerate((value, shift(value, "c"))):
            for z in range(array.shape[0]):

                def row(dy=dy, dx=dx):
                    y = (lax.axis_index("y") + dy) % 2
                    x = (lax.axis_index("x") + dx) % 2
                    return (y * 2 + x) * rows

                def col(dc=dc, at=low + z):
                    c = (lax.axis_index("c") + dc) % CORES
                    return at * CORES * cols + c * cols

                plan.append((len(pieces), z, row, col))
            pieces.append(array)
    return pieces, plan, corner_low


def gather_heads(own, beside):
    rows, cols = own.shape
    if lax.axis_size("y") != 2:
        full = lax.all_gather(own, ("y", "c"), axis=1, tiled=True)
        return [full], [(0, None, 0, 0)], beside()
    over = shift(own, "y")
    mate = shift(own, "c")
    done = beside()
    over, *done = tie(over, *done)
    pieces, plan = [own, mate, over, shift(over, "c")], []
    for number in range(len(pieces)):

        def col(dy=number // 2, dc=number % 2):
            y = (lax.axis_index("y") + dy) % 2
            c = (lax.axis_index("c") + dc) % CORES
            return (y * CORES + c) * cols

        plan.append((number, None, 0, col))
    return pieces, plan, done


def gather_x(own):
    if lax.axis_size("x") != 2:
        return lax.all_gather(own, "x", axis=0, tiled=False)
    return jnp.stack(order(own, shift(own, "x"), lax.axis_index("x")))


def gather_table(own):
    if lax.axis_size("y") != 2:
        return lax.all_gather(own, ("y", "c"), axis=1, tiled=True)
    pair = jnp.concatenate(order(own, shift(own, "c"), lax.axis_index("c")), axis=1)
    return jnp.concatenate(order(pair, shift(pair, "y"), lax.axis_index("y")), axis=1)


def gather_stats(own):
    if lax.axis_size("y") != 2 or lax.axis_size("x") != 2:
        return lax.all_gather(lax.psum(own, "c"), ("y", "x"), axis=0, tiled=True)
    own = own + shift(own, "c")
    pair = jnp.concatenate(order(own, shift(own, "x"), lax.axis_index("x")))
    return jnp.concatenate(order(pair, shift(pair, "y"), lax.axis_index("y")))


def shards(
    attention,
    out_proj,
    residual,
    norm_gain,
    router,
    routes,
    cotangent,
    gate_weight,
    up_weight,
    down_weight,
):
    n_y, n_z, n_x = lax.axis_size("y"), lax.axis_size("z"), lax.axis_size("x")
    at_y, at_c = lax.axis_index("y"), lax.axis_index("c")
    at_z, at_x = lax.axis_index("z"), lax.axis_index("x")
    tok = attention.shape[0]
    cap = tok * 9 // 16
    parts = n_z // n_y
    feats = residual.shape[1]
    width = feats * n_y * CORES
    cols = width // (n_z * CORES)
    rows_total = n_z * n_x * cap
    swaps = [swap_pairs(n_y, n_z, n_x, parts, turn) for turn in range(parts)]
    gate_w, up_w, down_w = gate_weight[0], up_weight[0], down_weight[0]

    far_proj = shift(out_proj, "x") if n_x == 2 else None
    line = jnp.zeros((n_z * tok, attention.shape[1]), BF)
    arrived = [(shift(attention, "z", step), step) for step in range(1, n_z)]
    for block, step in [(attention, 0)] + arrived:
        at = (at_z + n_z - step) % n_z * tok
        line = lax.dynamic_update_slice(line, block, (at, 0))

    ids = jnp.arange(EXPERTS, dtype=jnp.int32)
    slot_ids = jnp.arange(cap, dtype=jnp.int32)
    pair = jnp.arange(tok * 2, dtype=jnp.int32)
    before = (pair[None, :] < pair[:, None]).astype(BF)

    def places(named):
        blocks = named.shape[0]
        hits = (named.reshape(blocks, tok * 2)[:, :, None] == ids).astype(BF)
        earlier = jnp.einsum("pq,bqe->bpe", before, hits, preferred_element_type=F32)
        slots = jnp.sum(earlier * hits.astype(F32), axis=2).astype(jnp.int32)
        slots = slots.reshape(blocks, tok, 2)
        either = None
        for k in range(2):
            same = named[:, None, None, :, k] == ids[None, :, None, None]
            same = same & (slots[:, None, None, :, k] == slot_ids[None, None, :, None])
            either = same if either is None else either | same
        return either.astype(BF)

    own_place = places(routes[None]).reshape(EXPERTS * cap, tok)

    both_ids = (routes[:, :1] + routes[:, 1:]).astype(BF)
    cot_wide = jnp.concatenate([cotangent, jnp.broadcast_to(both_ids, (tok, LANES))], axis=1)
    cot_send = dot32(own_place, cot_wide, ((1,), (0,))).astype(BF)
    cot_got = lax.all_to_all(
        cot_send.reshape(n_z, cap, feats + LANES), "z", split_axis=0, concat_axis=0, tiled=True
    )
    res_after, cot_got = tie(residual, cot_got)
    cot_rows = gather_x(cot_got).reshape(n_x, n_y, parts * cap, feats + LANES)
    cot_rows = cot_rows.transpose(1, 0, 2, 3).reshape(rows_total, feats + LANES)

    route_cols = jnp.pad(routes.astype(BF), ((0, 0), (0, LANES - 2)))
    res_cut = res_after.reshape(tok, parts, cols)
    res_got = [
        lax.ppermute(
            jnp.concatenate([pick(res_cut, (turn + at_z) % parts, 1), route_cols], axis=1),
            ALL_AXES,
            swaps[turn],
        )
        for turn in range(parts)
    ]
    if parts == 2:
        res_mid = jnp.stack(order(res_got[0], res_got[1], at_c))
    else:
        res_mid = res_got[0][None]
    mid_place = places(res_mid[:, :, cols : cols + 2].astype(jnp.int32))
    res_mid = res_mid[:, :, :cols].reshape(parts * tok, cols)
    table = jnp.concatenate([norm_gain.astype(F32)[None, :], router.T], axis=0)
    table = gather_table(table)
    gain_all = table[:1]
    gain_mid = lax.dynamic_slice(gain_all, (0, (at_z * CORES + at_c) * cols), (1, cols))
    own_table = pick(table.reshape(1 + EXPERTS, n_z, CORES, cols), at_c, 2)
    weight = 1.0 / (own_table[0] * own_table[0])
    weight = weight[:, None, :]
    high = lax.reduce_precision(own_table[1:], 8, 7)
    middle = lax.reduce_precision(own_table[1:] - high, 8, 7)
    low = own_table[1:] - high - middle
    split = jnp.concatenate([high, middle, low], axis=0).astype(BF).transpose(1, 0, 2)
    split = jnp.pad(split, ((0, 0), (0, LANES - split.shape[1]), (0, 0)))

    line, res_mid = tie(line, res_mid)
    if n_x == 2:
        near = dot32(line, out_proj, ((1,), (0,)))
        far = dot32(line, far_proj, ((1,), (0,)))
        keep, give = order(near, far, at_c ^ at_x)
    else:
        wide = lax.all_gather(out_proj, "x", axis=1, tiled=True)
        both = dot32(line, wide, ((1,), (0,))).reshape(-1, CORES, cols)
        keep, give = pick(both, at_c, 1), pick(both, 1 - at_c, 1)
    summed = keep + shift(give.astype(BF), "c").astype(F32)
    summed = summed.reshape(n_y, parts * tok, cols)
    proj_mid = pick(summed, at_y)
    for step in range(1, n_y):
        outgoing = pick(summed, (at_y + step) % n_y).astype(BF)
        proj_mid = proj_mid + shift(outgoing, "y", step).astype(F32)
    scaled = ((res_mid.astype(F32) + proj_mid) * gain_mid).astype(BF)

    x_send = jnp.einsum(
        "best,btd->ebsd",
        mid_place,
        scaled.reshape(parts, tok, cols),
        preferred_element_type=F32,
    ).astype(BF)
    x_send, cot_rows, split, weight = tie(x_send, cot_rows, split, weight)
    x_got = lax.all_to_all(
        x_send.reshape(n_z, parts * cap, cols), "z", split_axis=0, concat_axis=0, tiled=True
    )
    pieces, plan, _ = gather_plane(x_got)

    stats = gather_stats(row_stats(x_got, split, weight))

    back, x_got = tie(proj_mid.astype(BF), x_got)
    back = back.reshape(parts, tok, cols)
    got = [
        lax.ppermute(
            pick(back, (at_c + parts - turn) % parts), ALL_AXES, [(b, a) for a, b in swaps[turn]]
        )
        for turn in range(parts)
    ]
    if parts == 2:
        proj = jnp.concatenate(order(got[0], got[1], at_z % 2), axis=1)
    else:
        proj = got[0]
    stats, proj = tie(stats, proj)

    hidden_cols = gate_w.shape[1]
    near_heads = (at_y + 1 + jnp.arange(n_y, dtype=jnp.int32)) % n_y * CORES
    dh_give = hidden_grad_part(near_heads + 1 - at_c, cot_rows, down_w, hidden_cols)
    dh_got = shift(dh_give, "c")
    dh_keep = hidden_grad_part(near_heads + at_c, cot_rows, down_w, hidden_cols)
    hidden_grad = dh_keep[n_y - 1].astype(F32) + dh_got[n_y - 1].astype(F32)
    for step in range(1, n_y):
        outgoing = dh_keep[step - 1].astype(F32) + dh_got[step - 1].astype(F32)
        outgoing, stats, *pieces = tie(outgoing.astype(BF), stats, *pieces)
        hidden_grad = hidden_grad + shift(outgoing, "y", step).astype(F32)
    hidden_grad = hidden_grad.astype(BF)

    hidden_local, a_val, b_val, scale, x_rows = forward(
        pieces, plan, gate_w, up_w, stats, cot_rows, feats // LANES
    )
    hidden_local, hidden_grad = tie(hidden_local, hidden_grad)
    pieces, plan, (grad_gate, grad_up) = gather_heads(
        hidden_local, lambda: gate_up_grads(x_rows, a_val, b_val, hidden_grad, scale)
    )

    size = parts * cap
    split_rows = (n_y, n_x, size) if size % 16 == 0 else None
    half = feats // 2 if feats % 512 == 0 else feats
    outs = []
    for start in range(0, feats, half):
        if start == 0:
            partial_out, hidden_all = down_first(
                pieces, plan, down_w, half, rows_total, split_rows
            )
        else:
            partial_out = down_next(hidden_all, down_w, start, half, split_rows)
        if split_rows is None:
            partial_out = partial_out.reshape(n_y, n_x, size, half).transpose(1, 0, 2, 3)
            partial_out = partial_out.reshape(n_x, n_y * size, half)
        out_rows = pick(partial_out, at_x).astype(F32)
        for step in range(1, n_x):
            outgoing = pick(partial_out, (at_x + step) % n_x)
            out_rows = out_rows + shift(outgoing, "x", step).astype(F32)
        out_rows = out_rows.astype(BF).reshape(n_z, cap, half)
        if start == 0:
            out_rows, cot_late = tie(out_rows, cot_rows)
        outs.append(
            lax.all_to_all(out_rows, "z", split_axis=0, concat_axis=0, tiled=True)
        )
    returned = jnp.concatenate(outs, axis=2).reshape(EXPERTS * cap, feats)
    grad_down = down_grad(hidden_all, cot_late, feats)

    state = residual.astype(F32) + proj.astype(F32)
    layer_out = state + dot32(own_place, returned, ((0,), (0,)))
    return (layer_out, grad_gate[None], grad_up[None], grad_down[None])


def solution(mesh):
    heads, owners = mesh.shape["head"], mesh.shape["expert"]
    fine = Mesh(
        mesh.devices.reshape(heads // CORES, CORES, EXPERTS, owners // EXPERTS), ALL_AXES
    )
    head, expert = ("y", "c"), ("z", "x")
    return jax.shard_map(
        shards,
        mesh=fine,
        in_specs=(
            P(expert, head),
            P(head, expert),
            P(expert, head),
            P(head),
            P(head, None),
            P(expert, None),
            P(expert, head),
            P(expert, None, head),
            P(expert, None, head),
            P(expert, None, head),
        ),
        out_specs=(
            P(expert, head),
            P(expert, None, head),
            P(expert, None, head),
            P(expert, None, head),
        ),
        check_vma=False,
    )
```

time: 769 us -> 299 us (0.39)
  waiting for transfers between devices: 593 us -> 94.9 us
  matrix products: 126 us -> 11.6 us
  Pallas kernels: 0 us -> 96.5 us
  starting transfers between devices: 16.6 us -> 67 us
  between operations: 14 us -> 1.49 us
  other arithmetic: 3.84 us -> 12.8 us
    all_gather x3 -> x0, waiting for transfers between devices: 409 us -> none  [the longest x1 367 us: shards(): lax.all_gather(out_proj, 'expert', axis=1, tiled=True)]
    all_to_all x3 -> x4, waiting for transfers between devices: 158 us -> 28.6 us  [the longest x1 14 us: shards(): lax.all_to_all(x_send.reshape(n_z, parts * cap, cols), 'z', split_axis=0,...]
    dot_general x14 -> x7, matrix products: 126 us -> 11.6 us  [the longest x4 10.7 us: dot32(): return lax.dot_general(a, b, (dims, ((), ())), preferred_element_type=F32)]
    pallas_call x0 -> x8, Pallas kernels: none -> 96.5 us  [the longest x1 26.7 us: gate_up_grads(): pl.pallas_call(gate_up_kernel, grid=(width // tile,), in_specs=[pl.BlockS...]
    ppermute x0 -> x32, waiting for transfers between devices: none -> 66.3 us  [the longest x28 63.3 us: shift(): lax.ppermute(value, axis, [(i, (i + step) % size) for i in range(size)])]
    ppermute x0 -> x32, starting transfers between devices: none -> 50.9 us  [the longest x28 49.5 us: shift(): lax.ppermute(value, axis, [(i, (i + step) % size) for i in range(size)])]
    reduce_scatter x2 -> x0, waiting for transfers between devices: 25.9 us -> none  [the longest x1 25.9 us: shards(): lax.psum_scatter(partial_value.astype(jnp.bfloat16), 'head', scatter_dime...]
    all_to_all x3 -> x4, starting transfers between devices: 16.2 us -> 16.1 us  [the longest x2 7.06 us: shards(): lax.all_to_all(out_rows, 'z', split_axis=0, concat_axis=0, tiled=True)]
  transfers between devices with their start and end apart: 8 -> 36, of which waited for: 7 -> 15; matrix products, arithmetic and copies ran while one was open for 13% -> 10% of each run, Pallas kernels for 0% -> 30%
where the time goes in v1:
time: 299 us; the launch traced here: 297 us
  Pallas kernels  96.5 us (32%)
  waiting for transfers between devices  94.9 us (32%)
  starting transfers between devices  67 us (22%)
  local copies, waits for them, and re-layouts  13 us (4%)
  other arithmetic  12.8 us (4%)
  matrix products  11.6 us (4%)
    ppermute x28, waiting for transfers between devices, shift(): lax.ppermute(value, axis, [(i, (i + step) % size) for i in range(size)])  63.3 us
    ppermute x28, starting transfers between devices, shift(): lax.ppermute(value, axis, [(i, (i + step) % size) for i in range(size)])  49.5 us
    pallas_call x1, Pallas kernels, gate_up_grads(): pl.pallas_call(gate_up_kernel, grid=(width // tile,), in_specs=[pl.BlockS...  26.7 us
    pallas_call x1, Pallas kernels, forward(): pl.pallas_call(functools.partial(forward_kernel, plan, len(pieces), width...  23.7 us
    pallas_call x2, Pallas kernels, hidden_grad_part(): pl.pallas_call(hidden_grad_kernel, grid_spec=pltpu.PrefetchScalarGridSpec...  15.8 us
    all_to_all x1, waiting for transfers between devices, shards(): lax.all_to_all(x_send.reshape(n_z, parts * cap, cols), 'z', split_axis=0,...  14 us
    pallas_call x1, Pallas kernels, down_grad(): pl.pallas_call(down_grad_kernel, grid=(hidden // tile,), in_specs=[pl.Blo...  14 us
    dot_general x4, matrix products, dot32(): return lax.dot_general(a, b, (dims, ((), ())), preferred_element_type=F32)  10.7 us
  transfers between devices with their start and end apart: 36, of which 15 were waited for; matrix products, arithmetic and copies ran while one was open for 10% of the time, Pallas kernels for 30%

profile of v1, /device:TPU:0, one launch (start us, length us, event | category | flops | bytes accessed | tf_op | source)
XLA Modules:
  0.0 297.3 jit_solution(18348828679246012224)
XLA Ops:
  0.6 3.1 %collective-permute-start = (bf16[128,1536]{1,0:T(8,128)(2,1)}, bf16[128,1536]{1,0:T(8,128)(2,1)}, u32[]{:S(2)}, u32[]{:S(2)}) collective-permute-start(bf16[128,1536]{1,0:T(8,128)(2,1)} %param.10), channel_id=1, source_target_pairs={{0,2},{2,4},{4,6},{6,0},{1,3},{3,5},{5,7},{7,1},{8,10},{10,12},{12... | collective-permute-start | bytes 1179656 | tf_op jit(solution)/shard_map/ppermute | solution.py:22
  12.1 2.3 convolution_convert_fusion
  14.4 3.6 %all-to-all-start = ((bf16[4,72,1664]{2,1,0:T(8,128)(2,1)}), bf16[4,72,1664]{2,1,0:T(8,128)(2,1)S(1)}, u32[]{:S(2)}, u32[]{:S(2)}) async-start(bf16[4,72,1664]{2,1,0:T(8,128)(2,1)} %bitcast.7), calls=%async_computation | async-start | bytes 1916928 | tf_op jit(solution)/shard_map/all_to_all | solution.py:538
  22.3 3.4 %collective-permute-done.9 = f32[5,3072]{1,0:T(8,128)S(1)} collective-permute-done((f32[5,3072]{1,0:T(8,128)S(1)}, f32[5,3072]{1,0:T(8,128)S(1)}, u32[]{:S(2)}, u32[]{:S(2)}) %collective-permute-start.9) | collective-permute-done | bytes 61472 | tf_op jit(solution)/shard_map/ppermute | solution.py:22
  28.8 22.0 %collective-permute-done.1 = bf16[128,1536]{1,0:T(8,128)(2,1)} collective-permute-done((bf16[128,1536]{1,0:T(8,128)(2,1)}, bf16[128,1536]{1,0:T(8,128)(2,1)}, u32[]{:S(2)}, u32[]{:S(2)}) %collective-permute-start.1) | collective-permute-done | bytes 393248 | tf_op jit(solution)/shard_map/ppermute | solution.py:22
  51.8 9.0 %all-to-all-done = bf16[4,72,1664]{2,1,0:T(8,128)(2,1)S(1)} async-done(((bf16[4,72,1664]{2,1,0:T(8,128)(2,1)}), bf16[4,72,1664]{2,1,0:T(8,128)(2,1)S(1)}, u32[]{:S(2)}, u32[]{:S(2)}) %all-to-all-start) | async-done | bytes 958496 | tf_op jit(solution)/shard_map/all_to_all | solution.py:538
  65.6 2.9 collective-permute-done.4
  69.4 3.0 %fusion.47 = f32[512,768]{1,0:T(8,128)S(1)} fusion(bf16[512,1536]{1,0:T(8,128)(2,1)S(1)} %constant_dynamic-update-slice_fusion, bf16[1536,768]{1,0:T(8,128)(2,1)} %param.11), kind=kOutput, calls=%fused_computation.132 | convolution fusion | flops 1207959552 | bytes 5505024 | tf_op jit(solution)/shard_map/dot_general | solution.py:49
  72.5 3.0 %select_convert_fusion = (bf16[512,768]{1,0:T(8,128)(2,1)S(1)}, f32[512,768]{1,0:T(8,128)S(1)}) fusion(f32[512,768]{1,0:T(8,128)S(1)} %fusion.47, pred[]{:T(512)S(6)} %eq.265, bf16[512,1536]{1,0:T(8,128)(2,1)S(1)} %constant_dynamic-update-slice_fusion, bf16[1536,768]{1,0:T(8,128)(2,1)} %collective-permute-done.5), kind=kOutput, calls=%fused_computation.8 | convolution fusion | flops 1208352768 | bytes 7864321 | tf_op jit(solution)/shard_map/dot_general | solution.py:49
  75.5 6.9 %collective-permute-start.6 = (bf16[512,768]{1,0:T(8,128)(2,1)S(1)}, bf16[512,768]{1,0:T(8,128)(2,1)S(1)}, u32[]{:S(2)}, u32[]{:S(2)}) collective-permute-start(bf16[512,768]{1,0:T(8,128)(2,1)S(1)} %get-tuple-element.115), channel_id=1, source_target_pairs={{0,8},{8,0},{1,9},{9,1},{2,10},{10,2},{3,11},{11,3},{4,12},{12,4},... | collective-permute-start | bytes 2359304 | tf_op jit(solution)/shard_map/ppermute | solution.py:22
  84.7 9.4 %collective-permute-start.7 = (bf16[256,768]{1,0:T(8,128)(2,1)S(1)}, bf16[256,768]{1,0:T(8,128)(2,1)S(1)}, u32[]{:S(2)}, u32[]{:S(2)}) collective-permute-start(bf16[256,768]{1,0:T(8,128)(2,1)S(1)} %fusion.19), channel_id=1, source_target_pairs={{0,16},{16,0},{1,17},{17,1},{2,18},{18,2},{3,19},{19,3},{4,20},{20... | collective-permute-start | bytes 1179656 | tf_op jit(solution)/shard_map/ppermute | solution.py:22
  95.7 7.8 %collective-permute-done.7 = bf16[256,768]{1,0:T(8,128)(2,1)S(1)} collective-permute-done((bf16[256,768]{1,0:T(8,128)(2,1)S(1)}, bf16[256,768]{1,0:T(8,128)(2,1)S(1)}, u32[]{:S(2)}, u32[]{:S(2)}) %collective-permute-start.7) | collective-permute-done | bytes 393248 | tf_op jit(solution)/shard_map/ppermute | solution.py:22
  105.0 5.4 %all-to-all-start.1 = ((bf16[4,144,768]{2,1,0:T(8,128)(2,1)}), bf16[4,144,768]{2,1,0:T(8,128)(2,1)S(1)}, u32[]{:S(2)}, u32[]{:S(2)}) async-start(bf16[4,144,768]{2,1,0:T(8,128)(2,1)} %bitcast.119), calls=%async_computation.1 | async-start | bytes 1769472 | tf_op jit(solution)/shard_map/all_to_all | solution.py:598
  110.4 7.9 %shard_map.131 = bf16[2,576,1024]{2,1,0:T(8,128)(2,1)} custom-call(s32[2]{0:T(128)S(1)} %add_subtract_fusion.heads, bf16[576,1664]{1,0:T(8,128)(2,1)S(1)} %bitcast.107, bf16[4096,1536]{1,0:T(8,128)(2,1)} %bitcast.111), custom_call_target="tpu_custom_call" | custom-call | flops 3623878656 | bytes 8650752 | tf_op jit(solution)/shard_map/pallas_call | solution.py:381
  118.3 14.0 %all-to-all-done.1.x.args_0_ = bf16[4,144,768]{2,1,0:T(8,128)(2,1)S(1)} async-done(((bf16[4,144,768]{2,1,0:T(8,128)(2,1)}), bf16[4,144,768]{2,1,0:T(8,128)(2,1)S(1)}, u32[]{:S(2)}, u32[]{:S(2)}) %all-to-all-start.1) | async-done | bytes 884768 | tf_op jit(solution)/shard_map/all_to_all | solution.py:598
  136.1 7.9 %shard_map.130 = bf16[2,576,1024]{2,1,0:T(8,128)(2,1)} custom-call(s32[2]{0:T(128)S(1)} %broadcast_add_fusion.heads, bf16[576,1664]{1,0:T(8,128)(2,1)S(1)} %bitcast.108, bf16[4096,1536]{1,0:T(8,128)(2,1)} %bitcast.112), custom_call_target="tpu_custom_call" | custom-call | flops 3623878656 | bytes 8650752 | tf_op jit(solution)/shard_map/pallas_call | solution.py:381
  145.4 9.4 %collective-permute-done.12 = f32[144,128]{1,0:T(8,128)S(1)} collective-permute-done((f32[144,128]{1,0:T(8,128)S(1)}, f32[144,128]{1,0:T(8,128)S(1)}, u32[]{:S(2)}, u32[]{:S(2)}) %collective-permute-start.12) | collective-permute-done | bytes 73760 | tf_op jit(solution)/shard_map/ppermute | solution.py:22
  159.1 8.0 %collective-permute-start.24 = (bf16[2,144,768]{2,1,0:T(8,128)(2,1)S(1)}, bf16[2,144,768]{2,1,0:T(8,128)(2,1)S(1)}, u32[]{:S(2)}, u32[]{:S(2)}) collective-permute-start(bf16[2,144,768]{2,1,0:T(8,128)(2,1)S(1)} %slice.105), channel_id=1, source_target_pairs={{0,16},{16,0},{1,17},{17,1},{2,18},{18,2},{3,19},{19,3},{4,20},{20... | collective-permute-start | bytes 1327112 | tf_op jit(solution)/shard_map/ppermute | solution.py:22
  169.9 4.5 %collective-permute-done.24.args_8_ = bf16[2,144,768]{2,1,0:T(8,128)(2,1)S(1)} collective-permute-done((bf16[2,144,768]{2,1,0:T(8,128)(2,1)S(1)}, bf16[2,144,768]{2,1,0:T(8,128)(2,1)S(1)}, u32[]{:S(2)}, u32[]{:S(2)}) %collective-permute-start.24) | collective-permute-done | bytes 442400 | tf_op jit(solution)/shard_map/ppermute | solution.py:22
  176.3 2.5 collective-permute-start.26
  178.8 23.7 %shard_map.132 = (bf16[576,1024]{1,0:T(8,128)(2,1)}, f32[576,1024]{1,0:T(8,128)}, f32[576,1024]{1,0:T(8,128)}, f32[576,128]{1,0:T(8,128)S(1)}, bf16[576,6144]{1,0:T(8,128)(2,1)}) custom-call(bf16[4,144,768]{2,1,0:T(8,128)(2,1)S(1)} %all-to-all-done.1.x.args_0_, bf16[4,144,768]{2,1,0:T(8,128)(2,1)S(1)} %collective-permute-done.17.args_1_, ...), custom_call_target="tpu_custom_call" | custom-call | flops 14495514624 | bytes 32243712 | tf_op jit(solution)/shard_map/pallas_call | solution.py:145
  202.6 2.9 collective-permute-done.26
  209.3 26.7 %shard_map.133 = (bf16[6144,1024]{1,0:T(8,128)(2,1)}, bf16[6144,1024]{1,0:T(8,128)(2,1)}) custom-call(bf16[576,6144]{1,0:T(8,128)(2,1)} %get-tuple-element.68.x, f32[576,1024]{1,0:T(8,128)S(1)} %copy-done.3, f32[576,1024]{1,0:T(8,128)} %get-tuple-element.70.b_in, bf16[576,1024]{1,0:T(8,128)(2,1)S(1)} %fusion.1.dh, f32[576,128]{1,0:T(8,128)S(1)} %get-tuple-element.72.scale), custom_call_target="tpu_custom_call" | custom-call | flops 14495514624 | bytes 38141952 | tf_op jit(solution)/shard_map/pallas_call | solution.py:206
  236.6 2.8 collective-permute-done.29.args_3_
  239.4 8.3 %shard_map.134 = (bf16[2,288,768]{2,1,0:T(8,128)(2,1)S(1)}, bf16[576,4096]{1,0:T(8,128)(2,1)}) custom-call(bf16[576,1024]{1,0:T(8,128)(2,1)S(1)} %copy-done.2, bf16[576,1024]{1,0:T(8,128)(2,1)S(1)} %collective-permute-done.27.args_1_, bf16[576,1024]{1,0:T(8,128)(2,1)} %collective-permute-done.28.args_2_, bf16[576,1024]{1,0:T(8,128)(2,1)} %collective-permute-done.29.args_3_, ...), custom_call_target="tpu_custom_call" | custom-call | flops 3623878656 | bytes 15728640 | tf_op jit(solution)/shard_map/pallas_call | solution.py:284
  249.3 7.4 %shard_map.135 = bf16[2,288,768]{2,1,0:T(8,128)(2,1)S(1)} custom-call(bf16[576,4096]{1,0:T(8,128)(2,1)} %get-tuple-element.78.hid, bf16[4096,1536]{1,0:T(8,128)(2,1)} %bitcast.114), custom_call_target="tpu_custom_call" | custom-call | flops 3623878656 | bytes 11010048 | tf_op jit(solution)/shard_map/pallas_call | solution.py:306
  261.2 3.6 %all-to-all-start.2 = ((bf16[4,72,768]{2,1,0:T(8,128)(2,1)}), bf16[4,72,768]{2,1,0:T(8,128)(2,1)S(1)}, u32[]{:S(2)}, u32[]{:S(2)}) async-start(bf16[4,72,768]{2,1,0:T(8,128)(2,1)} %bitcast.41), calls=%async_computation.2 | async-start | bytes 884736 | tf_op jit(solution)/shard_map/all_to_all | solution.py:661
  264.8 5.2 %collective-permute-done.31 = bf16[288,768]{1,0:T(8,128)(2,1)} collective-permute-done((bf16[288,768]{1,0:T(8,128)(2,1)}, bf16[288,768]{1,0:T(8,128)(2,1)}, u32[]{:S(2)}, u32[]{:S(2)}) %collective-permute-start.31) | collective-permute-done | bytes 442400 | tf_op jit(solution)/shard_map/ppermute | solution.py:22
  271.9 5.6 %all-to-all-done.2 = bf16[4,72,768]{2,1,0:T(8,128)(2,1)S(1)} async-done(((bf16[4,72,768]{2,1,0:T(8,128)(2,1)}), bf16[4,72,768]{2,1,0:T(8,128)(2,1)S(1)}, u32[]{:S(2)}, u32[]{:S(2)}) %all-to-all-start.2) | async-done | bytes 442400 | tf_op jit(solution)/shard_map/all_to_all | solution.py:661
  277.5 3.5 %all-to-all-start.3 = ((bf16[4,72,768]{2,1,0:T(8,128)(2,1)}), bf16[4,72,768]{2,1,0:T(8,128)(2,1)S(1)}, u32[]{:S(2)}, u32[]{:S(2)}) async-start(bf16[4,72,768]{2,1,0:T(8,128)(2,1)} %bitcast.44), calls=%async_computation.3 | async-start | bytes 884736 | tf_op jit(solution)/shard_map/all_to_all | solution.py:661
  281.0 14.0 %shard_map.136 = bf16[4096,1536]{1,0:T(8,128)(2,1)} custom-call(bf16[576,4096]{1,0:T(8,128)(2,1)} %get-tuple-element.78.hid, bf16[576,1664]{1,0:T(8,128)(2,1)S(1)} %bitcast.110), custom_call_target="tpu_custom_call" | custom-call | flops 7247757312 | bytes 17301504 | tf_op jit(solution)/shard_map/pallas_call | solution.py:326
  295.0 2.3 fusion
  (167 shorter events, 53.5 us)
Async XLA Ops:
  0.6 27.2 %collective-permute-start = (bf16[128,1536]{1,0:T(8,128)(2,1)}, bf16[128,1536]{1,0:T(8,128)(2,1)}, u32[]{:S(2)}, u32[]{:S(2)}) collective-permute-start(bf16[128,1536]{1,0:T(8,128)(2,1)} %param.10), channel_id=1, source_target_pairs={{0,2},{2,4},{4,6},{6,0},{1,3},{3,5},{5,7},{7,1},{8,10},{10,12},{12... | collective-permute-start | bytes 1179656 | tf_op jit(solution)/shard_map/ppermute | solution.py:22
  3.7 59.3 %collective-permute-start.2 = (bf16[128,1536]{1,0:T(8,128)(2,1)}, bf16[128,1536]{1,0:T(8,128)(2,1)}, u32[]{:S(2)}, u32[]{:S(2)}) collective-permute-start(bf16[128,1536]{1,0:T(8,128)(2,1)} %param.10), channel_id=1, source_target_pairs={{0,6},{2,0},{4,2},{6,4},{1,7},{3,1},{5,3},{7,5},{8,14},{10,8},{12,... | collective-permute-start | bytes 1179656 | tf_op jit(solution)/shard_map/ppermute | solution.py:22
  5.8 45.0 %collective-permute-start.1 = (bf16[128,1536]{1,0:T(8,128)(2,1)}, bf16[128,1536]{1,0:T(8,128)(2,1)}, u32[]{:S(2)}, u32[]{:S(2)}) collective-permute-start(bf16[128,1536]{1,0:T(8,128)(2,1)} %param.10), channel_id=1, source_target_pairs={{0,4},{2,6},{4,0},{6,2},{1,5},{3,7},{5,1},{7,3},{8,12},{10,14},{12... | collective-permute-start | bytes 1179656 | tf_op jit(solution)/shard_map/ppermute | solution.py:22
  8.2 12.5 %collective-permute-start.8 = (f32[5,1536]{1,0:T(8,128)S(1)}, f32[5,1536]{1,0:T(8,128)S(1)}, u32[]{:S(2)}, u32[]{:S(2)}) collective-permute-start(f32[5,1536]{1,0:T(8,128)S(1)} %pad_maximum_fusion.7), channel_id=1, source_target_pairs={{0,8},{8,0},{1,9},{9,1},{2,10},{10,2},{3,11},{11,3},{4,12},{12,4},... | collective-permute-start | bytes 92168 | tf_op jit(solution)/shard_map/ppermute | solution.py:22
  14.4 46.5 %all-to-all-start = ((bf16[4,72,1664]{2,1,0:T(8,128)(2,1)}), bf16[4,72,1664]{2,1,0:T(8,128)(2,1)S(1)}, u32[]{:S(2)}, u32[]{:S(2)}) async-start(bf16[4,72,1664]{2,1,0:T(8,128)(2,1)} %bitcast.7), calls=%async_computation | async-start | bytes 1916928 | tf_op jit(solution)/shard_map/all_to_all | solution.py:538
  18.1 54.4 %collective-permute-start.5 = (bf16[1536,768]{1,0:T(8,128)(2,1)}, bf16[1536,768]{1,0:T(8,128)(2,1)}, u32[]{:S(2)}, u32[]{:S(2)}) collective-permute-start(bf16[1536,768]{1,0:T(8,128)(2,1)} %param.11), channel_id=1, source_target_pairs={{0,1},{1,0},{2,3},{3,2},{4,5},{5,4},{6,7},{7,6},{8,9},{9,8},{10,11... | collective-permute-start | bytes 7077896 | tf_op jit(solution)/shard_map/ppermute | solution.py:22
  62.3 6.3 %collective-permute-start.4 = (bf16[128,896]{1,0:T(8,128)(2,1)S(1)}, bf16[128,896]{1,0:T(8,128)(2,1)S(1)}, u32[]{:S(2)}, u32[]{:S(2)}) collective-permute-start(bf16[128,896]{1,0:T(8,128)(2,1)S(1)} %get-tuple-element.111), channel_id=1, source_target_pairs={{0,8},{1,9},{2,0},{3,1},{4,24},{5,25},{6,16},{7,17},{8,10},{9,11},... | collective-permute-start | bytes 688136 | tf_op jit(solution)/shard_map/ppermute | solution.py:548
  62.3 6.2 %collective-permute-start.3 = (bf16[128,896]{1,0:T(8,128)(2,1)S(1)}, bf16[128,896]{1,0:T(8,128)(2,1)S(1)}, u32[]{:S(2)}, u32[]{:S(2)}) collective-permute-start(bf16[128,896]{1,0:T(8,128)(2,1)S(1)} %get-tuple-element.112), channel_id=1, source_target_pairs={{0,0},{1,1},{2,8},{3,9},{4,16},{5,17},{6,24},{7,25},{8,2},{9,3},{1... | collective-permute-start | bytes 688136 | tf_op jit(solution)/shard_map/ppermute | solution.py:548
  64.1 30.0 %collective-permute-start.10 = (bf16[4,72,1664]{2,1,0:T(8,128)(2,1)S(1)}, bf16[4,72,1664]{2,1,0:T(8,128)(2,1)}, u32[]{:S(2)}, u32[]{:S(2)}) collective-permute-start(bf16[4,72,1664]{2,1,0:T(8,128)(2,1)S(1)} %all-to-all-done), channel_id=1, source_target_pairs={{0,1},{1,0},{2,3},{3,2},{4,5},{5,4},{6,7},{7,6},{8,9},{9,8},{10,11... | collective-permute-start | bytes 2875400 | tf_op jit(solution)/shard_map/ppermute | solution.py:22
  75.5 8.8 %collective-permute-start.6 = (bf16[512,768]{1,0:T(8,128)(2,1)S(1)}, bf16[512,768]{1,0:T(8,128)(2,1)S(1)}, u32[]{:S(2)}, u32[]{:S(2)}) collective-permute-start(bf16[512,768]{1,0:T(8,128)(2,1)S(1)} %get-tuple-element.115), channel_id=1, source_target_pairs={{0,8},{8,0},{1,9},{9,1},{2,10},{10,2},{3,11},{11,3},{4,12},{12,4},... | collective-permute-start | bytes 2359304 | tf_op jit(solution)/shard_map/ppermute | solution.py:22
  84.7 18.8 %collective-permute-start.7 = (bf16[256,768]{1,0:T(8,128)(2,1)S(1)}, bf16[256,768]{1,0:T(8,128)(2,1)S(1)}, u32[]{:S(2)}, u32[]{:S(2)}) collective-permute-start(bf16[256,768]{1,0:T(8,128)(2,1)S(1)} %fusion.19), channel_id=1, source_target_pairs={{0,16},{16,0},{1,17},{17,1},{2,18},{18,2},{3,19},{19,3},{4,20},{20... | collective-permute-start | bytes 1179656 | tf_op jit(solution)/shard_map/ppermute | solution.py:22
  105.0 27.3 %all-to-all-start.1 = ((bf16[4,144,768]{2,1,0:T(8,128)(2,1)}), bf16[4,144,768]{2,1,0:T(8,128)(2,1)S(1)}, u32[]{:S(2)}, u32[]{:S(2)}) async-start(bf16[4,144,768]{2,1,0:T(8,128)(2,1)} %bitcast.119), calls=%async_computation.1 | async-start | bytes 1769472 | tf_op jit(solution)/shard_map/all_to_all | solution.py:598
  118.3 48.9 %collective-permute-start.16 = (bf16[2,576,1024]{2,1,0:T(8,128)(2,1)}, bf16[2,576,1024]{2,1,0:T(8,128)(2,1)}, u32[]{:S(2)}, u32[]{:S(2)}) collective-permute-start(bf16[2,576,1024]{2,1,0:T(8,128)(2,1)} %shard_map.131), channel_id=1, source_target_pairs={{0,8},{8,0},{1,9},{9,1},{2,10},{10,2},{3,11},{11,3},{4,12},{12,4},... | collective-permute-start | bytes 7077896 | tf_op jit(solution)/shard_map/ppermute | solution.py:22
  132.3 22.5 %collective-permute-start.20 = (bf16[4,144,768]{2,1,0:T(8,128)(2,1)S(1)}, bf16[4,144,768]{2,1,0:T(8,128)(2,1)S(1)}, u32[]{:S(2)}, u32[]{:S(2)}) collective-permute-start(bf16[4,144,768]{2,1,0:T(8,128)(2,1)S(1)} %all-to-all-done.1.x.args_0_), channel_id=1, source_target_pairs={{0,16},{16,0},{1,17},{17,1},{2,18},{18,2},{3,19},{19,3},{4,20},{20... | collective-permute-start | bytes 2654216 | tf_op jit(solution)/shard_map/ppermute | solution.py:22
  132.9 22.6 %collective-permute-start.18 = (bf16[4,144,768]{2,1,0:T(8,128)(2,1)S(1)}, bf16[4,144,768]{2,1,0:T(8,128)(2,1)S(1)}, u32[]{:S(2)}, u32[]{:S(2)}) collective-permute-start(bf16[4,144,768]{2,1,0:T(8,128)(2,1)S(1)} %all-to-all-done.1.x.args_0_), channel_id=1, source_target_pairs={{0,1},{1,0},{2,3},{3,2},{4,5},{5,4},{6,7},{7,6},{8,9},{9,8},{10,11... | collective-permute-start | bytes 2654216 | tf_op jit(solution)/shard_map/ppermute | solution.py:22
  136.1 7.9 %collective-permute-start.11 = (f32[144,128]{1,0:T(8,128)S(1)}, f32[144,128]{1,0:T(8,128)S(1)}, u32[]{:S(2)}, u32[]{:S(2)}) collective-permute-start(f32[144,128]{1,0:T(8,128)S(1)} %shard_map.129), channel_id=1, source_target_pairs={{0,8},{8,0},{1,9},{9,1},{2,10},{10,2},{3,11},{11,3},{4,12},{12,4},... | collective-permute-start | bytes 221192 | tf_op jit(solution)/shard_map/ppermute | solution.py:22
  144.0 10.7 %collective-permute-start.12 = (f32[144,128]{1,0:T(8,128)S(1)}, f32[144,128]{1,0:T(8,128)S(1)}, u32[]{:S(2)}, u32[]{:S(2)}) collective-permute-start(f32[144,128]{1,0:T(8,128)S(1)} %add.203), channel_id=1, source_target_pairs={{0,1},{1,0},{2,3},{3,2},{4,5},{5,4},{6,7},{7,6},{8,9},{9,8},{10,11... | collective-permute-start | bytes 221192 | tf_op jit(solution)/shard_map/ppermute | solution.py:22
  144.7 12.9 %collective-permute-start.14 = (bf16[128,768]{1,0:T(8,128)(2,1)S(1)}, bf16[128,768]{1,0:T(8,128)(2,1)S(1)}, u32[]{:S(2)}, u32[]{:S(2)}) collective-permute-start(bf16[128,768]{1,0:T(8,128)(2,1)S(1)} %get-tuple-element.96), channel_id=1, source_target_pairs={{0,0},{1,1},{8,2},{9,3},{16,4},{17,5},{24,6},{25,7},{2,8},{3,9},{1... | collective-permute-start | bytes 589832 | tf_op jit(solution)/shard_map/ppermute | solution.py:608
  154.8 21.4 %collective-permute-start.17 = (bf16[4,144,768]{2,1,0:T(8,128)(2,1)S(1)}, bf16[4,144,768]{2,1,0:T(8,128)(2,1)S(1)}, u32[]{:S(2)}, u32[]{:S(2)}) collective-permute-start(bf16[4,144,768]{2,1,0:T(8,128)(2,1)S(1)} %all-to-all-done.1.x.args_0_), channel_id=1, source_target_pairs={{0,8},{8,0},{1,9},{9,1},{2,10},{10,2},{3,11},{11,3},{4,12},{12,4},... | collective-permute-start | bytes 2654216 | tf_op jit(solution)/shard_map/ppermute | solution.py:22
  155.5 11.7 %collective-permute-start.13 = (f32[288,128]{1,0:T(8,128)S(1)}, f32[288,128]{1,0:T(8,128)S(1)}, u32[]{:S(2)}, u32[]{:S(2)}) collective-permute-start(f32[288,128]{1,0:T(8,128)S(1)} %pad_maximum_fusion.4), channel_id=1, source_target_pairs={{0,16},{16,0},{1,17},{17,1},{2,18},{18,2},{3,19},{19,3},{4,20},{20... | collective-permute-start | bytes 442376 | tf_op jit(solution)/shard_map/ppermute | solution.py:22
  157.6 12.3 %collective-permute-start.22 = (bf16[2,144,768]{2,1,0:T(8,128)(2,1)S(1)}, bf16[2,144,768]{2,1,0:T(8,128)(2,1)S(1)}, u32[]{:S(2)}, u32[]{:S(2)}) collective-permute-start(bf16[2,144,768]{2,1,0:T(8,128)(2,1)S(1)} %slice.104), channel_id=1, source_target_pairs={{0,1},{1,0},{2,3},{3,2},{4,5},{5,4},{6,7},{7,6},{8,9},{9,8},{10,11... | collective-permute-start | bytes 1327112 | tf_op jit(solution)/shard_map/ppermute | solution.py:22
  159.1 15.3 %collective-permute-start.24 = (bf16[2,144,768]{2,1,0:T(8,128)(2,1)S(1)}, bf16[2,144,768]{2,1,0:T(8,128)(2,1)S(1)}, u32[]{:S(2)}, u32[]{:S(2)}) collective-permute-start(bf16[2,144,768]{2,1,0:T(8,128)(2,1)S(1)} %slice.105), channel_id=1, source_target_pairs={{0,16},{16,0},{1,17},{17,1},{2,18},{18,2},{3,19},{19,3},{4,20},{20... | collective-permute-start | bytes 1327112 | tf_op jit(solution)/shard_map/ppermute | solution.py:22
  167.2 9.1 %collective-permute-start.21 = (bf16[4,144,768]{2,1,0:T(8,128)(2,1)S(1)}, bf16[4,144,768]{2,1,0:T(8,128)(2,1)S(1)}, u32[]{:S(2)}, u32[]{:S(2)}) collective-permute-start(bf16[4,144,768]{2,1,0:T(8,128)(2,1)S(1)} %collective-permute-done.20.args_4_), channel_id=1, source_target_pairs={{0,8},{8,0},{1,9},{9,1},{2,10},{10,2},{3,11},{11,3},{4,12},{12,4},... | collective-permute-start | bytes 2654216 | tf_op jit(solution)/shard_map/ppermute | solution.py:22
  167.3 9.0 %collective-permute-start.19 = (bf16[4,144,768]{2,1,0:T(8,128)(2,1)S(1)}, bf16[4,144,768]{2,1,0:T(8,128)(2,1)S(1)}, u32[]{:S(2)}, u32[]{:S(2)}) collective-permute-start(bf16[4,144,768]{2,1,0:T(8,128)(2,1)S(1)} %collective-permute-done.18.args_2_), channel_id=1, source_target_pairs={{0,8},{8,0},{1,9},{9,1},{2,10},{10,2},{3,11},{11,3},{4,12},{12,4},... | collective-permute-start | bytes 2654216 | tf_op jit(solution)/shard_map/ppermute | solution.py:22
  169.9 6.3 %collective-permute-start.23 = (bf16[2,144,768]{2,1,0:T(8,128)(2,1)S(1)}, bf16[2,144,768]{2,1,0:T(8,128)(2,1)S(1)}, u32[]{:S(2)}, u32[]{:S(2)}) collective-permute-start(bf16[2,144,768]{2,1,0:T(8,128)(2,1)S(1)} %collective-permute-done.22.args_6_), channel_id=1, source_target_pairs={{0,8},{8,0},{1,9},{9,1},{2,10},{10,2},{3,11},{11,3},{4,12},{12,4},... | collective-permute-start | bytes 1327112 | tf_op jit(solution)/shard_map/ppermute | solution.py:22
  176.3 29.2 %collective-permute-start.26 = (bf16[576,1024]{1,0:T(8,128)(2,1)S(1)}, bf16[576,1024]{1,0:T(8,128)(2,1)S(1)}, u32[]{:S(2)}, u32[]{:S(2)}) collective-permute-start(bf16[576,1024]{1,0:T(8,128)(2,1)S(1)} %fusion.3), channel_id=1, source_target_pairs={{0,16},{16,0},{1,17},{17,1},{2,18},{18,2},{3,19},{19,3},{4,20},{20... | collective-permute-start | bytes 3538952 | tf_op jit(solution)/shard_map/ppermute | solution.py:22
  207.5 28.6 %collective-permute-start.28 = (bf16[576,1024]{1,0:T(8,128)(2,1)S(1)}, bf16[576,1024]{1,0:T(8,128)(2,1)}, u32[]{:S(2)}, u32[]{:S(2)}) collective-permute-start(bf16[576,1024]{1,0:T(8,128)(2,1)S(1)} %copy-done.2), channel_id=1, source_target_pairs={{0,16},{16,0},{1,17},{17,1},{2,18},{18,2},{3,19},{19,3},{4,20},{20... | collective-permute-start | bytes 3538952 | tf_op jit(solution)/shard_map/ppermute | solution.py:22
  209.3 27.3 %collective-permute-start.27 = (bf16[576,1024]{1,0:T(8,128)(2,1)S(1)}, bf16[576,1024]{1,0:T(8,128)(2,1)S(1)}, u32[]{:S(2)}, u32[]{:S(2)}) collective-permute-start(bf16[576,1024]{1,0:T(8,128)(2,1)S(1)} %copy-done.2), channel_id=1, source_target_pairs={{0,8},{8,0},{1,9},{9,1},{2,10},{10,2},{3,11},{11,3},{4,12},{12,4},... | collective-permute-start | bytes 3538952 | tf_op jit(solution)/shard_map/ppermute | solution.py:22
  247.8 12.5 %collective-permute-start.30 = (bf16[288,768]{1,0:T(8,128)(2,1)S(1)}, bf16[288,768]{1,0:T(8,128)(2,1)S(1)}, u32[]{:S(2)}, u32[]{:S(2)}) collective-permute-start(bf16[288,768]{1,0:T(8,128)(2,1)S(1)} %dynamic-slice_bitcast_fusion.1), channel_id=1, source_target_pairs={{0,1},{1,0},{2,3},{3,2},{4,5},{5,4},{6,7},{7,6},{8,9},{9,8},{10,11... | collective-permute-start | bytes 1327112 | tf_op jit(solution)/shard_map/ppermute | solution.py:22
  257.6 12.5 %collective-permute-start.31 = (bf16[288,768]{1,0:T(8,128)(2,1)}, bf16[288,768]{1,0:T(8,128)(2,1)}, u32[]{:S(2)}, u32[]{:S(2)}) collective-permute-start(bf16[288,768]{1,0:T(8,128)(2,1)} %dynamic-slice_bitcast_fusion), channel_id=1, source_target_pairs={{0,1},{1,0},{2,3},{3,2},{4,5},{5,4},{6,7},{7,6},{8,9},{9,8},{10,11... | collective-permute-start | bytes 1327112 | tf_op jit(solution)/shard_map/ppermute | solution.py:22
  261.2 16.3 %all-to-all-start.2 = ((bf16[4,72,768]{2,1,0:T(8,128)(2,1)}), bf16[4,72,768]{2,1,0:T(8,128)(2,1)S(1)}, u32[]{:S(2)}, u32[]{:S(2)}) async-start(bf16[4,72,768]{2,1,0:T(8,128)(2,1)} %bitcast.41), calls=%async_computation.2 | async-start | bytes 884736 | tf_op jit(solution)/shard_map/all_to_all | solution.py:661
  277.5 17.5 %all-to-all-start.3 = ((bf16[4,72,768]{2,1,0:T(8,128)(2,1)}), bf16[4,72,768]{2,1,0:T(8,128)(2,1)S(1)}, u32[]{:S(2)}, u32[]{:S(2)}) async-start(bf16[4,72,768]{2,1,0:T(8,128)(2,1)} %bitcast.44), calls=%async_computation.3 | async-start | bytes 884736 | tf_op jit(solution)/shard_map/all_to_all | solution.py:661
  (23 other events, 237.3 us)

commit v2 on v1

v2 whole, which is shorter than its diff:
```python
import functools

import jax
import jax.numpy as jnp
from jax import lax
from jax.experimental import pallas as pl
from jax.experimental.pallas import tpu as pltpu
from jax.sharding import Mesh, PartitionSpec as P

EPSILON = 1e-05
EXPERTS = 4
CORES = 2
LANES = 128
VMEM = 50 * 2**20
BF = jnp.bfloat16
F32 = jnp.float32
ALL_AXES = ("y", "c", "z", "x")


def shift(value, axis, step=1):
    size = lax.axis_size(axis)
    return lax.ppermute(value, axis, [(i, (i + step) % size) for i in range(size)])


def pick(stack, index, axis=0):
    return lax.dynamic_index_in_dim(stack, index, axis, keepdims=False)


def tie(*values):
    return lax.optimization_barrier(values)


def after(value, *others):
    return tie(value, *others)[0]


def swap_pairs(n_y, n_z, n_x, parts, turn):
    pairs = []
    for y in range(n_y):
        for c in range(CORES):
            for z in range(n_z):
                for x in range(n_x):
                    piece = (y * CORES + c) * parts + (turn + z) % parts
                    to_z, to_c = piece // CORES, piece % CORES
                    to_y = z // parts
                    source = ((y * CORES + c) * n_z + z) * n_x + x
                    target = ((to_y * CORES + to_c) * n_z + to_z) * n_x + x
                    pairs.append((source, target))
    return pairs


def dot32(a, b, dims):
    return lax.dot_general(a, b, (dims, ((), ())), preferred_element_type=F32)


def sigmoid(value):
    return 1.0 / (1.0 + jnp.exp(-value))


def order(mine, other, index):
    first = index == 0
    return jnp.where(first, mine, other), jnp.where(first, other, mine)


def place_copies(plan, refs, scratch, sems):
    copies = []
    for number, (ref, lead, row, col) in enumerate(plan):
        source = refs[ref] if lead is None else refs[ref].at[lead]
        n_rows, n_cols = source.shape
        row = pl.multiple_of(row(), 16) if callable(row) else row
        col = pl.multiple_of(col(), LANES) if callable(col) else col
        copies.append(
            pltpu.make_async_copy(
                source,
                scratch.at[pl.ds(row, n_rows), pl.ds(col, n_cols)],
                sems.at[number],
            )
        )
    return copies


def whole(shape):
    return pl.BlockSpec(shape, lambda *_: (0,) * len(shape))


def column_tile(cols):
    return 256 if cols % 256 == 0 else cols


def params():
    return pltpu.CompilerParams(vmem_limit_bytes=VMEM)


def cost(flops, bytes_accessed, transcendentals=0):
    return pl.CostEstimate(
        flops=flops, bytes_accessed=bytes_accessed, transcendentals=transcendentals
    )


def forward_kernel(plan, n_refs, width, *args):
    refs = args[:n_refs]
    gate_w, up_w, split, weight, hid, u_out, v_out, logits, x_out = args[n_refs:-4]
    x_all, inv, sems, sem = args[-4:]
    step = pl.program_id(0)
    rows = x_all.shape[0]
    keep = pltpu.make_async_copy(x_all, x_out, sem)

    @pl.when(step == 0)
    def _():
        copies = place_copies(plan, refs, x_all, sems)
        for copy in copies:
            copy.start()
        for copy in copies:
            copy.wait()
        keep.start()
        chunk = 48

        def squares(index, carry):
            at = pl.multiple_of(index * chunk, 16)
            total = jnp.zeros((chunk, LANES), F32)
            for k in range(width // LANES):
                part = x_all[pl.ds(at, chunk), k * LANES : (k + 1) * LANES].astype(F32)
                total = total + part * part * weight[:, k * LANES : (k + 1) * LANES]
            mean = jnp.sum(total, axis=1, keepdims=True) / width
            inv[pl.ds(at, chunk), :] = jnp.broadcast_to(
                lax.rsqrt(mean + EPSILON), (chunk, LANES)
            )
            return carry

        lax.fori_loop(0, rows // chunk, squares, 0)
        logits[...] = dot32(x_all[...], split[...], ((1,), (1,))) * inv[...]

    x = x_all[...]
    a = jnp.dot(x, gate_w[...], preferred_element_type=F32)
    b = jnp.dot(x, up_w[...], preferred_element_type=F32)
    inverse = inv[:, :1]
    a = a * inverse
    b = b * inverse
    s = sigmoid(a)
    act = a * s
    hid[...] = (act * b).astype(BF)
    u_out[...] = (b * (s + act * (1.0 - s)) * inverse).astype(BF)
    v_out[...] = (act * inverse).astype(BF)

    @pl.when(step == pl.num_programs(0) - 1)
    def _():
        keep.wait()


def forward(pieces, plan, rows, gate_w, up_w, split, weight):
    width, cols = gate_w.shape
    tile = 256 if cols % 256 == 0 else cols
    anywhere = pl.BlockSpec(memory_space=pl.ANY)
    return pl.pallas_call(
        functools.partial(forward_kernel, plan, len(pieces), width),
        grid=(cols // tile,),
        in_specs=[anywhere] * len(pieces)
        + [
            pl.BlockSpec((width, tile), lambda j: (0, j)),
            pl.BlockSpec((width, tile), lambda j: (0, j)),
            whole((LANES, width)),
            whole((1, width)),
        ],
        out_specs=[pl.BlockSpec((rows, tile), lambda j: (0, j))] * 3
        + [whole((rows, LANES)), anywhere],
        out_shape=[jax.ShapeDtypeStruct((rows, cols), BF)] * 3
        + [
            jax.ShapeDtypeStruct((rows, LANES), F32),
            jax.ShapeDtypeStruct((rows, width), BF),
        ],
        scratch_shapes=[
            pltpu.VMEM((rows, width), BF),
            pltpu.VMEM((rows, LANES), F32),
            pltpu.SemaphoreType.DMA((len(plan),)),
            pltpu.SemaphoreType.DMA,
        ],
        compiler_params=pltpu.CompilerParams(vmem_limit_bytes=VMEM),
        cost_estimate=cost(4 * rows * width * cols, 4 * width * cols + 2 * rows * width),
    )(*pieces, gate_w, up_w, split, weight)


def prob_kernel(logits, meta, prob):
    lane = lax.broadcasted_iota(jnp.int32, logits.shape, 1)
    own = lax.axis_index("z")
    other = meta[...].astype(F32).astype(jnp.int32) - own
    expert = lane % EXPERTS
    sign = (expert == own).astype(F32) - (expert == other).astype(F32)
    sign = jnp.where(lane < 3 * EXPERTS, sign, 0.0)
    gap = jnp.sum(logits[...] * sign, axis=1, keepdims=True)
    prob[...] = jnp.broadcast_to(sigmoid(gap), prob.shape)


def row_probs(logits, cot_rows, meta_block):
    rows = logits.shape[0]
    return pl.pallas_call(
        prob_kernel,
        grid=(1,),
        in_specs=[
            whole((rows, LANES)),
            pl.BlockSpec((rows, LANES), lambda j: (0, meta_block)),
        ],
        out_specs=whole((rows, LANES)),
        out_shape=jax.ShapeDtypeStruct((rows, LANES), F32),
        compiler_params=params(),
        cost_estimate=cost(20 * rows * LANES, 10 * rows * LANES, rows),
    )(logits, cot_rows)


def weight_grad_kernel(n_terms, *args):
    x, factor, prob = args[:3]
    terms = args[3 : 3 + n_terms]
    out, grad = args[3 + n_terms :]

    @pl.when(pl.program_id(0) == 0)
    def _():
        for k in range(factor.shape[1] // LANES):
            at = slice(k * LANES, (k + 1) * LANES)
            dh = terms[0][:, at].astype(F32)
            for term in terms[1:]:
                dh = dh + term[:, at].astype(F32)
            grad[:, at] = (dh * prob[...] * factor[:, at].astype(F32)).astype(BF)

    out[...] = dot32(x[...], grad[...], ((0,), (0,))).astype(BF)


def weight_grad(x_rows, factor, prob, stacks, terms):
    rows, width = x_rows.shape
    cols = factor.shape[1]
    tile = 512
    last = [
        pl.BlockSpec((pl.squeezed, rows, cols), lambda j, at=stack.shape[0] - 1: (at, 0, 0))
        for stack in stacks
    ]
    return pl.pallas_call(
        functools.partial(weight_grad_kernel, len(stacks) + len(terms)),
        grid=(width // tile,),
        in_specs=[
            pl.BlockSpec((rows, tile), lambda j: (0, j)),
            whole((rows, cols)),
            whole((rows, LANES)),
        ]
        + last
        + [whole((rows, cols))] * len(terms),
        out_specs=pl.BlockSpec((tile, cols), lambda j: (j, 0)),
        out_shape=jax.ShapeDtypeStruct((width, cols), BF),
        scratch_shapes=[pltpu.VMEM((rows, cols), BF)],
        compiler_params=params(),
        cost_estimate=cost(
            2 * rows * width * cols, 2 * width * cols + 2 * rows * width + 8 * rows * cols
        ),
    )(x_rows, factor, prob, *stacks, *terms)


def down_store(value, out, split_rows):
    if split_rows is None:
        out[...] = value
        return
    n_y, n_x, size = split_rows
    for y in range(n_y):
        for x in range(n_x):
            at = (y * n_x + x) * size
            out[x, y * size : (y + 1) * size, :] = value[at : at + size]


def down_kernel(plan, n_refs, split_rows, *args):
    refs = args[:n_refs]
    down_w, prob, out, hid_out, hid, sems, sem = args[n_refs:]
    step = pl.program_id(0)
    keep = pltpu.make_async_copy(hid, hid_out, sem)

    @pl.when(step == 0)
    def _():
        copies = place_copies(plan, refs, hid, sems)
        for copy in copies:
            copy.start()
        for copy in copies:
            copy.wait()
        keep.start()

    value = jnp.dot(hid[...], down_w[...], preferred_element_type=F32) * prob[:, :1]
    down_store(value.astype(BF), out, split_rows)

    @pl.when(step == pl.num_programs(0) - 1)
    def _():
        keep.wait()


def down_next_kernel(split_rows, hid, down_w, prob, out):
    value = jnp.dot(hid[...], down_w[...], preferred_element_type=F32) * prob[:, :1]
    down_store(value.astype(BF), out, split_rows)


def down_specs(rows, hidden, tile, feats, base, split_rows):
    weight = pl.BlockSpec((hidden, tile), lambda j: (0, j + base))
    if split_rows is None:
        out = pl.BlockSpec((rows, tile), lambda j: (0, j))
        shape = jax.ShapeDtypeStruct((rows, feats), BF)
    else:
        n_y, n_x, size = split_rows
        out = pl.BlockSpec((n_x, n_y * size, tile), lambda j: (0, 0, j))
        shape = jax.ShapeDtypeStruct((n_x, n_y * size, feats), BF)
    return weight, out, shape


def down_first(pieces, plan, down_w, prob, feats, split_rows):
    hidden, rows = down_w.shape[0], prob.shape[0]
    tile = column_tile(feats)
    anywhere = pl.BlockSpec(memory_space=pl.ANY)
    weight, out, shape = down_specs(rows, hidden, tile, feats, 0, split_rows)
    return pl.pallas_call(
        functools.partial(down_kernel, plan, len(pieces), split_rows),
        grid=(feats // tile,),
        in_specs=[anywhere] * len(pieces) + [weight, whole((rows, LANES))],
        out_specs=[out, anywhere],
        out_shape=[shape, jax.ShapeDtypeStruct((rows, hidden), BF)],
        scratch_shapes=[
            pltpu.VMEM((rows, hidden), BF),
            pltpu.SemaphoreType.DMA((len(plan),)),
            pltpu.SemaphoreType.DMA,
        ],
        compiler_params=params(),
        cost_estimate=cost(
            2 * rows * hidden * feats, 2 * hidden * feats + 4 * rows * hidden
        ),
    )(*pieces, down_w, prob)


def down_next(hidden_all, down_w, prob, start, feats, split_rows):
    rows, hidden = hidden_all.shape
    tile = column_tile(feats)
    weight, out, shape = down_specs(rows, hidden, tile, feats, start // tile, split_rows)
    return pl.pallas_call(
        functools.partial(down_next_kernel, split_rows),
        grid=(feats // tile,),
        in_specs=[whole((rows, hidden)), weight, whole((rows, LANES))],
        out_specs=out,
        out_shape=shape,
        compiler_params=params(),
        cost_estimate=cost(
            2 * rows * hidden * feats, 2 * hidden * feats + 2 * rows * hidden
        ),
    )(hidden_all, down_w, prob)


def down_grad_kernel(n_pieces, steps, *args):
    pieces = args[1 : 1 + n_pieces]
    cot, prob, out, scaled = args[1 + n_pieces], args[2 + n_pieces], args[-2], args[-1]
    step = pl.program_id(0)

    @pl.when(step == 0)
    def _():
        for k in range(scaled.shape[1] // LANES):
            at = slice(k * LANES, (k + 1) * LANES)
            scaled[:, at] = (cot[:, at].astype(F32) * prob[...]).astype(BF)

    for number in range(n_pieces):

        @pl.when(step // steps == number)
        def _(piece=pieces[number]):
            out[...] = dot32(piece[...], scaled[...], ((0,), (0,))).astype(BF)


def down_grad(heads, pieces, cot_rows, prob, feats):
    rows, cols = pieces[0].shape
    tile = 512 if cols % 512 == 0 else cols
    steps = cols // tile
    n_pieces = len(pieces)

    def piece_spec(number):
        return pl.BlockSpec(
            (rows, tile), lambda i, heads: (0, jnp.clip(i - number * steps, 0, steps - 1))
        )

    return pl.pallas_call(
        functools.partial(down_grad_kernel, n_pieces, steps),
        grid_spec=pltpu.PrefetchScalarGridSpec(
            num_scalar_prefetch=1,
            grid=(n_pieces * steps,),
            in_specs=[piece_spec(number) for number in range(n_pieces)]
            + [pl.BlockSpec((rows, feats), lambda i, heads: (0, 0)), whole((rows, LANES))],
            out_specs=pl.BlockSpec(
                (tile, feats), lambda i, heads: (heads[i // steps] * steps + i % steps, 0)
            ),
            scratch_shapes=[pltpu.VMEM((rows, feats), BF)],
        ),
        out_shape=jax.ShapeDtypeStruct((n_pieces * cols, feats), BF),
        compiler_params=params(),
        cost_estimate=cost(
            2 * rows * n_pieces * cols * feats, 2 * n_pieces * cols * (feats + rows)
        ),
    )(heads, *pieces, cot_rows, prob)


def hidden_grad_kernel(n_heads, heads, cot, down_w, give, keep):
    value = dot32(cot[...], down_w[...], ((1,), (1,))).astype(BF)

    @pl.when(pl.program_id(0) < n_heads)
    def _():
        give[...] = value

    @pl.when(pl.program_id(0) >= n_heads)
    def _():
        keep[...] = value


def hidden_grad_parts(heads, cot_rows, down_w, cols):
    rows, feats = cot_rows.shape[0], down_w.shape[1]
    tile = 512 if cols % 512 == 0 else cols
    steps = cols // tile
    n_heads = heads.shape[0] // 2

    def give_at(i, j, heads):
        first = i < n_heads
        return jnp.where(first, i, n_heads - 1), 0, jnp.where(first, j, steps - 1)

    def keep_at(i, j, heads):
        first = i < n_heads
        return jnp.where(first, 0, i - n_heads), 0, jnp.where(first, 0, j)

    block = (pl.squeezed, rows, tile)
    return pl.pallas_call(
        functools.partial(hidden_grad_kernel, n_heads),
        grid_spec=pltpu.PrefetchScalarGridSpec(
            num_scalar_prefetch=1,
            grid=(2 * n_heads, steps),
            in_specs=[
                pl.BlockSpec((rows, feats), lambda i, j, heads: (0, 0)),
                pl.BlockSpec((tile, feats), lambda i, j, heads: (heads[i] * steps + j, 0)),
            ],
            out_specs=[pl.BlockSpec(block, give_at), pl.BlockSpec(block, keep_at)],
        ),
        out_shape=[jax.ShapeDtypeStruct((n_heads, rows, cols), BF)] * 2,
        compiler_params=params(),
        cost_estimate=cost(
            4 * rows * feats * cols * n_heads, 4 * n_heads * cols * (feats + rows)
        ),
    )(heads, cot_rows, down_w)


def gather_plane(own):
    n_y, n_x, n_z = lax.axis_size("y"), lax.axis_size("x"), own.shape[0]
    rows, cols = own.shape[1:]
    if n_y != 2 or n_x != 2 or rows % 16:
        full = lax.all_gather(own, ("y", "x", "c"), axis=0, tiled=False)
        full = full.reshape(n_y, n_x, CORES, n_z, rows, cols).transpose(0, 1, 4, 3, 2, 5)
        full = full.reshape(n_y * n_x * rows, n_z * CORES * cols)
        return [full], [(0, None, 0, 0)], full
    half = n_z // 2
    side = shift(own, "x")
    over = shift(own, "y")
    corner_low = shift(over[:half], "x")
    corner_high = shift(side[half:], "y")
    found = [
        (own, 0, 0, 0),
        (side, 0, 1, 0),
        (over, 1, 0, 0),
        (corner_low, 1, 1, 0),
        (corner_high, 1, 1, half),
    ]
    pieces, plan = [], []
    for value, dy, dx, low in found:
        for dc, array in enumerate((value, shift(value, "c"))):
            for z in range(array.shape[0]):

                def row(dy=dy, dx=dx):
                    y = (lax.axis_index("y") + dy) % 2
                    x = (lax.axis_index("x") + dx) % 2
                    return (y * 2 + x) * rows

                def col(dc=dc, at=low + z):
                    c = (lax.axis_index("c") + dc) % CORES
                    return at * CORES * cols + c * cols

                plan.append((len(pieces), z, row, col))
            pieces.append(array)
    return pieces, plan, corner_low


def gather_heads(own, beside):
    rows, cols = own.shape
    if lax.axis_size("y") != 2:
        full = lax.all_gather(own, ("y", "c"), axis=1, tiled=True)
        return [full], [(0, None, 0, 0)], beside(own)
    over = shift(own, "y")
    mate = shift(own, "c")
    done = beside(mate)
    over = after(over, done[-1])
    pieces, plan = [own, mate, over, shift(over, "c")], []
    for number in range(len(pieces)):

        def col(dy=number // 2, dc=number % 2):
            y = (lax.axis_index("y") + dy) % 2
            c = (lax.axis_index("c") + dc) % CORES
            return (y * CORES + c) * cols

        plan.append((number, None, 0, col))
    return pieces, plan, done


def gather_x(own):
    if lax.axis_size("x") != 2:
        return lax.all_gather(own, "x", axis=0, tiled=False)
    return jnp.stack(order(own, shift(own, "x"), lax.axis_index("x")))


def gather_table(own):
    if lax.axis_size("y") != 2:
        return lax.all_gather(own, ("y", "c"), axis=1, tiled=True)
    pair = jnp.concatenate(order(own, shift(own, "c"), lax.axis_index("c")), axis=1)
    return jnp.concatenate(order(pair, shift(pair, "y"), lax.axis_index("y")), axis=1)


def shards(
    attention,
    out_proj,
    residual,
    norm_gain,
    router,
    routes,
    cotangent,
    gate_weight,
    up_weight,
    down_weight,
):
    n_y, n_z, n_x = lax.axis_size("y"), lax.axis_size("z"), lax.axis_size("x")
    at_y, at_c = lax.axis_index("y"), lax.axis_index("c")
    at_z, at_x = lax.axis_index("z"), lax.axis_index("x")
    tok = attention.shape[0]
    cap = tok * 9 // 16
    parts = n_z // n_y
    feats = residual.shape[1]
    width = feats * n_y * CORES
    cols = width // (n_z * CORES)
    rows_total = n_z * n_x * cap
    swaps = [swap_pairs(n_y, n_z, n_x, parts, turn) for turn in range(parts)]
    gate_w, up_w, down_w = gate_weight[0], up_weight[0], down_weight[0]

    far_proj = shift(out_proj, "x") if n_x == 2 else None
    line = jnp.zeros((n_z * tok, attention.shape[1]), BF)
    arrived = [(shift(attention, "z", step), step) for step in range(1, n_z)]
    for block, step in [(attention, 0)] + arrived:
        at = (at_z + n_z - step) % n_z * tok
        line = lax.dynamic_update_slice(line, block, (at, 0))

    ids = jnp.arange(EXPERTS, dtype=jnp.int32)
    slot_ids = jnp.arange(cap, dtype=jnp.int32)
    pair = jnp.arange(tok * 2, dtype=jnp.int32)
    before = (pair[None, :] < pair[:, None]).astype(BF)

    def places(named):
        blocks = named.shape[0]
        hits = (named.reshape(blocks, tok * 2)[:, :, None] == ids).astype(BF)
        earlier = jnp.einsum("pq,bqe->bpe", before, hits, preferred_element_type=F32)
        slots = jnp.sum(earlier * hits.astype(F32), axis=2).astype(jnp.int32)
        slots = slots.reshape(blocks, tok, 2)
        either = None
        for k in range(2):
            same = named[:, None, None, :, k] == ids[None, :, None, None]
            same = same & (slots[:, None, None, :, k] == slot_ids[None, None, :, None])
            either = same if either is None else either | same
        return either.astype(BF)

    own_place = places(routes[None]).reshape(EXPERTS * cap, tok)

    route_cols = jnp.pad(routes.astype(BF), ((0, 0), (0, LANES - 2)))
    res_cut = residual.reshape(tok, parts, cols)
    res_got = [
        lax.ppermute(
            jnp.concatenate([pick(res_cut, (turn + at_z) % parts, 1), route_cols], axis=1),
            ALL_AXES,
            swaps[turn],
        )
        for turn in range(parts)
    ]
    if parts == 2:
        res_mid = jnp.stack(order(res_got[0], res_got[1], at_c))
    else:
        res_mid = res_got[0][None]
    mid_place = places(res_mid[:, :, cols : cols + 2].astype(jnp.int32))
    res_mid = res_mid[:, :, :cols].reshape(parts * tok, cols)
    table = jnp.concatenate([norm_gain.astype(F32)[None, :], router.T], axis=0)
    table = gather_table(table)
    gain_all = table[:1]
    gain_mid = lax.dynamic_slice(gain_all, (0, (at_z * CORES + at_c) * cols), (1, cols))
    weight = 1.0 / (gain_all * gain_all)
    high = lax.reduce_precision(table[1:], 8, 7)
    middle = lax.reduce_precision(table[1:] - high, 8, 7)
    low = table[1:] - high - middle
    split = jnp.concatenate([high, middle, low], axis=0).astype(BF)
    split = jnp.pad(split, ((0, LANES - split.shape[0]), (0, 0)))

    if n_x == 2:
        near = dot32(line, out_proj, ((1,), (0,)))
        far = dot32(line, far_proj, ((1,), (0,)))
        keep, give = order(near, far, at_c ^ at_x)
    else:
        wide = lax.all_gather(out_proj, "x", axis=1, tiled=True)
        both = dot32(line, wide, ((1,), (0,))).reshape(-1, CORES, cols)
        keep, give = pick(both, at_c, 1), pick(both, 1 - at_c, 1)
    summed = keep + shift(give.astype(BF), "c").astype(F32)
    summed = summed.reshape(n_y, parts * tok, cols)
    proj_mid = pick(summed, at_y)
    for step in range(1, n_y):
        outgoing = pick(summed, (at_y + step) % n_y).astype(BF)
        proj_mid = proj_mid + shift(outgoing, "y", step).astype(F32)
    scaled = ((res_mid.astype(F32) + proj_mid) * gain_mid).astype(BF)

    x_send = jnp.einsum(
        "best,btd->ebsd",
        mid_place,
        scaled.reshape(parts, tok, cols),
        preferred_element_type=F32,
    ).astype(BF)
    x_got = lax.all_to_all(
        x_send.reshape(n_z, parts * cap, cols), "z", split_axis=0, concat_axis=0, tiled=True
    )

    back = after(proj_mid.astype(BF), x_got)
    back = back.reshape(parts, tok, cols)
    got = [
        lax.ppermute(
            pick(back, (at_c + parts - turn) % parts), ALL_AXES, [(b, a) for a, b in swaps[turn]]
        )
        for turn in range(parts)
    ]
    if parts == 2:
        proj = jnp.concatenate(order(got[0], got[1], at_z % 2), axis=1)
    else:
        proj = got[0]

    pieces, plan, corner = gather_plane(x_got)
    pieces[0], proj = tie(pieces[0], proj)

    both_ids = (routes[:, :1] + routes[:, 1:]).astype(BF)
    cot_wide = jnp.concatenate([cotangent, jnp.broadcast_to(both_ids, (tok, LANES))], axis=1)
    cot_send = dot32(own_place, cot_wide, ((1,), (0,))).astype(BF)
    cot_send = after(cot_send, x_got)
    cot_got = lax.all_to_all(
        cot_send.reshape(n_z, cap, feats + LANES), "z", split_axis=0, concat_axis=0, tiled=True
    )
    cot_got = after(cot_got, corner, *pieces[-2:])
    cot_rows = gather_x(cot_got).reshape(n_x, n_y, parts * cap, feats + LANES)
    cot_rows = cot_rows.transpose(1, 0, 2, 3).reshape(rows_total, feats + LANES)

    hidden_cols = gate_w.shape[1]
    hidden_local, u_val, v_val, logits, x_rows = forward(
        pieces, plan, rows_total, gate_w, up_w, split, weight
    )

    prob = row_probs(logits, cot_rows, feats // LANES)
    near_heads = (at_y + 1 + jnp.arange(n_y, dtype=jnp.int32)) % n_y * CORES

    heads = jnp.concatenate([near_heads + 1 - at_c, near_heads + at_c])

    def beside(mate):
        return hidden_grad_parts(heads, after(cot_rows, mate), down_w, hidden_cols)

    pieces, plan, (dh_give, dh_keep) = gather_heads(hidden_local, beside)
    dh_got = shift(dh_give, "c")
    going = [
        (dh_keep[step - 1].astype(F32) + dh_got[step - 1].astype(F32)).astype(BF)
        for step in range(1, n_y)
    ]

    size = parts * cap
    split_rows = (n_y, n_x, size) if size % 16 == 0 else None
    half = feats // 2 if feats % 512 == 0 else feats
    outs, sums = [], []
    for start in range(0, feats, half):
        if start == 0:
            partial_out, hidden_all = down_first(
                pieces, plan, down_w, prob, half, split_rows
            )
        else:
            hidden_all = after(hidden_all, *going)
            partial_out = down_next(hidden_all, down_w, prob, start, half, split_rows)
        if split_rows is None:
            partial_out = partial_out.reshape(n_y, n_x, size, half).transpose(1, 0, 2, 3)
            partial_out = partial_out.reshape(n_x, n_y * size, half)
        out_rows = pick(partial_out, at_x).astype(F32)
        for step in range(1, n_x):
            outgoing = pick(partial_out, (at_x + step) % n_x)
            out_rows = out_rows + shift(outgoing, "x", step).astype(F32)
        out_rows = out_rows.astype(BF).reshape(n_z, cap, half)
        sums.append(out_rows)
        outs.append(
            lax.all_to_all(out_rows, "z", split_axis=0, concat_axis=0, tiled=True)
        )
    dh_terms = [shift(value, "y", step + 1) for step, value in enumerate(going)]
    returned = jnp.concatenate(outs, axis=2).reshape(EXPERTS * cap, feats)
    heads = jnp.zeros((1,), jnp.int32)
    cot_late = cot_rows
    grad_down = down_grad(heads, [hidden_all], cot_late, prob, feats)
    parts_of = (dh_keep, dh_got), [after(term, sums[0]) for term in dh_terms]
    grad_gate = weight_grad(x_rows, u_val, prob, *parts_of)
    parts_of = (dh_keep, dh_got), [after(term, sums[-1]) for term in dh_terms]
    grad_up = weight_grad(x_rows, v_val, prob, *parts_of)

    state = residual.astype(F32) + proj.astype(F32)
    layer_out = state + dot32(own_place, returned, ((0,), (0,)))
    return (layer_out, grad_gate[None], grad_up[None], grad_down[None])


def solution(mesh):
    heads, owners = mesh.shape["head"], mesh.shape["expert"]
    fine = Mesh(
        mesh.devices.reshape(heads // CORES, CORES, EXPERTS, owners // EXPERTS), ALL_AXES
    )
    head, expert = ("y", "c"), ("z", "x")
    return jax.shard_map(
        shards,
        mesh=fine,
        in_specs=(
            P(expert, head),
            P(head, expert),
            P(expert, head),
            P(head),
            P(head, None),
            P(expert, None),
            P(expert, head),
            P(expert, None, head),
            P(expert, None, head),
            P(expert, None, head),
        ),
        out_specs=(
            P(expert, head),
            P(expert, None, head),
            P(expert, None, head),
            P(expert, None, head),
        ),
        check_vma=False,
    )
```

time: 299 us -> 316 us (1.057)
  waiting for transfers between devices: 94.9 us -> 116 us
  starting transfers between devices: 67 us -> 47.3 us
  Pallas kernels: 96.5 us -> 110 us
    ppermute x28 -> x25, waiting for transfers between devices: 63.3 us -> 88.5 us  [shift(): lax.ppermute(value, axis, [(i, (i + step) % size) for i in range(size)])]
    ppermute x28 -> x25, starting transfers between devices: 49.5 us -> 26.4 us  [shift(): lax.ppermute(value, axis, [(i, (i + step) % size) for i in range(size)])]
    all_to_all x1, waiting for transfers between devices: 9.05 us -> 0.33 us  [shards(): lax.all_to_all(cot_send.reshape(n_z, cap, feats + LANES), 'z', split_axis...]
    pallas_call x5, Pallas kernels: 57.1 us -> 65.7 us  [the longest x2 37.1 us: weight_grad(): pl.pallas_call(functools.partial(weight_grad_kernel, len(stacks) + len(te...]
    all_to_all x1, waiting for transfers between devices: 14 us -> 22.3 us  [shards(): lax.all_to_all(x_send.reshape(n_z, parts * cap, cols), 'z', split_axis=0,...]
    pallas_call x1, Pallas kernels: 23.7 us -> 28.8 us  [forward(): pl.pallas_call(functools.partial(forward_kernel, plan, len(pieces), width...]
    unnamed x40 -> x33, local copies, waits for them, and re-layouts: 2.16 us -> 6.59 us
  transfers between devices with their start and end apart: 36 -> 33, of which waited for: 15 -> 14; matrix products, arithmetic and copies ran while one was open for 10% -> 10% of each run, Pallas kernels for 30% -> 23%
where the time goes in v2:
time: 316 us; the launch traced here: 314 us
  waiting for transfers between devices  116 us (37%)
  Pallas kernels  110 us (35%)
  starting transfers between devices  47.3 us (15%)
  local copies, waits for them, and re-layouts  14.7 us (5%)
  other arithmetic  13.3 us (4%)
  matrix products  10.8 us (3%)
    ppermute x25, waiting for transfers between devices, shift(): lax.ppermute(value, axis, [(i, (i + step) % size) for i in range(size)])  88.5 us
    pallas_call x2, Pallas kernels, weight_grad(): pl.pallas_call(functools.partial(weight_grad_kernel, len(stacks) + len(te...  37.1 us
    pallas_call x1, Pallas kernels, forward(): pl.pallas_call(functools.partial(forward_kernel, plan, len(pieces), width...  28.8 us
    ppermute x25, starting transfers between devices, shift(): lax.ppermute(value, axis, [(i, (i + step) % size) for i in range(size)])  26.4 us
    all_to_all x1, waiting for transfers between devices, shards(): lax.all_to_all(x_send.reshape(n_z, parts * cap, cols), 'z', split_axis=0,...  22.3 us
    pallas_call x1, Pallas kernels, down_grad(): pl.pallas_call(functools.partial(down_grad_kernel, n_pieces, steps), grid...  14.5 us
    pallas_call x1, Pallas kernels, hidden_grad_parts(): pl.pallas_call(functools.partial(hidden_grad_kernel, n_heads), grid_spec=...  14 us
    dot_general x4, matrix products, dot32(): return lax.dot_general(a, b, (dims, ((), ())), preferred_element_type=F32)  9.95 us
  transfers between devices with their start and end apart: 33, of which 14 were waited for; matrix products, arithmetic and copies ran while one was open for 10% of the time, Pallas kernels for 23%

profile of v2, /device:TPU:0, one launch (start us, length us, event | category | flops | bytes accessed | tf_op | source)
XLA Modules:
  0.0 314.2 jit_solution(6621299048915355417)
XLA Ops:
  0.6 3.1 collective-permute-start.2
  3.7 2.6 collective-permute-start.3
  15.8 2.5 collective-permute-done.9
  21.1 12.0 %collective-permute-done.3 = bf16[128,1536]{1,0:T(8,128)(2,1)} collective-permute-done((bf16[128,1536]{1,0:T(8,128)(2,1)}, bf16[128,1536]{1,0:T(8,128)(2,1)}, u32[]{:S(2)}, u32[]{:S(2)}) %collective-permute-start.3) | collective-permute-done | bytes 393248 | tf_op jit(solution)/shard_map/ppermute | solution.py:22
  35.5 24.6 %collective-permute-done.5 = bf16[1536,768]{1,0:T(8,128)(2,1)} collective-permute-done((bf16[1536,768]{1,0:T(8,128)(2,1)}, bf16[1536,768]{1,0:T(8,128)(2,1)}, u32[]{:S(2)}, u32[]{:S(2)}) %collective-permute-start.5) | collective-permute-done | bytes 2359328 | tf_op jit(solution)/shard_map/ppermute | solution.py:22
  60.1 4.5 %select_convert_fusion = (bf16[512,768]{1,0:T(8,128)(2,1)}, f32[512,768]{1,0:T(8,128)}) fusion(f32[512,768]{1,0:T(8,128)S(1)} %fusion.52, pred[]{:T(512)S(6)} %eq.238, bf16[512,1536]{1,0:T(8,128)(2,1)S(1)} %constant_dynamic-update-slice_fusion, bf16[1536,768]{1,0:T(8,128)(2,1)} %collective-permute-done.5), kind=kOutput, calls=%fused_computation.12 | convolution fusion | flops 1208352768 | bytes 7864321 | tf_op jit(solution)/shard_map/dot_general | solution.py:53
  69.3 9.7 %collective-permute-done.7 = bf16[256,768]{1,0:T(8,128)(2,1)S(1)} collective-permute-done((bf16[256,768]{1,0:T(8,128)(2,1)S(1)}, bf16[256,768]{1,0:T(8,128)(2,1)S(1)}, u32[]{:S(2)}, u32[]{:S(2)}) %collective-permute-start.7) | collective-permute-done | bytes 393248 | tf_op jit(solution)/shard_map/ppermute | solution.py:22
  80.6 3.5 %all-to-all-start = ((bf16[4,144,768]{2,1,0:T(8,128)(2,1)}), bf16[4,144,768]{2,1,0:T(8,128)(2,1)S(1)}, u32[]{:S(2)}, u32[]{:S(2)}) async-start(bf16[4,144,768]{2,1,0:T(8,128)(2,1)} %bitcast.16), calls=%async_computation | async-start | bytes 1769472 | tf_op jit(solution)/shard_map/all_to_all | solution.py:614
  84.8 22.3 %all-to-all-done.args_0_ = bf16[4,144,768]{2,1,0:T(8,128)(2,1)S(1)} async-done(((bf16[4,144,768]{2,1,0:T(8,128)(2,1)}), bf16[4,144,768]{2,1,0:T(8,128)(2,1)S(1)}, u32[]{:S(2)}, u32[]{:S(2)}) %all-to-all-start) | async-done | bytes 884768 | tf_op jit(solution)/shard_map/all_to_all | solution.py:614
  110.8 3.0 collective-permute-start.10
  113.8 4.4 %all-to-all-start.1 = ((bf16[4,72,1664]{2,1,0:T(8,128)(2,1)}), bf16[4,72,1664]{2,1,0:T(8,128)(2,1)}, u32[]{:S(2)}, u32[]{:S(2)}) async-start(bf16[4,72,1664]{2,1,0:T(8,128)(2,1)} %bitcast.29), calls=%async_computation.1 | async-start | bytes 1916928 | tf_op jit(solution)/shard_map/all_to_all | solution.py:638
  119.9 15.1 %collective-permute-done.15.args_4_ = bf16[4,144,768]{2,1,0:T(8,128)(2,1)} collective-permute-done((bf16[4,144,768]{2,1,0:T(8,128)(2,1)S(1)}, bf16[4,144,768]{2,1,0:T(8,128)(2,1)}, u32[]{:S(2)}, u32[]{:S(2)}) %collective-permute-start.15) | collective-permute-done | bytes 884768 | tf_op jit(solution)/shard_map/ppermute | solution.py:22
  138.7 2.7 collective-permute-start.19
  143.2 3.3 %collective-permute-done.17.args_6_ = bf16[2,144,768]{2,1,0:T(8,128)(2,1)S(1)} collective-permute-done((bf16[2,144,768]{2,1,0:T(8,128)(2,1)S(1)}, bf16[2,144,768]{2,1,0:T(8,128)(2,1)S(1)}, u32[]{:S(2)}, u32[]{:S(2)}) %collective-permute-start.17) | collective-permute-done | bytes 442400 | tf_op jit(solution)/shard_map/ppermute | solution.py:22
  146.5 2.9 collective-permute-done.19.args_8_
  151.6 2.1 collective-permute-start.23
  153.7 28.8 %shard_map.129 = (bf16[576,1024]{1,0:T(8,128)(2,1)}, bf16[576,1024]{1,0:T(8,128)(2,1)}, bf16[576,1024]{1,0:T(8,128)(2,1)}, f32[576,128]{1,0:T(8,128)S(1)}, bf16[576,6144]{1,0:T(8,128)(2,1)}) custom-call(bf16[4,144,768]{2,1,0:T(8,128)(2,1)S(1)} %all-to-all-done.args_0_, bf16[4,144,768]{2,1,0:T(8,128)(2,1)S(1)} %collective-permute-done.12.args_1_, ...), custom_call_target="tpu_custom_call" | custom-call | flops 14495514624 | bytes 32243712 | tf_op jit(solution)/shard_map/pallas_call | solution.py:154
  187.5 14.0 %shard_map.130 = (bf16[2,576,1024]{2,1,0:T(8,128)(2,1)}, bf16[2,576,1024]{2,1,0:T(8,128)(2,1)}) custom-call(s32[4]{0:T(128)S(1)} %pad_add_fusion.heads, bf16[576,1664]{1,0:T(8,128)(2,1)S(1)} %bitcast.94, bf16[4096,1536]{1,0:T(8,128)(2,1)} %bitcast.97), custom_call_target="tpu_custom_call" | custom-call | flops 7247757312 | bytes 17301504 | tf_op jit(solution)/shard_map/pallas_call | solution.py:421
  201.5 10.5 %collective-permute-done.22.args_2_ = bf16[576,1024]{1,0:T(8,128)(2,1)} collective-permute-done((bf16[576,1024]{1,0:T(8,128)(2,1)}, bf16[576,1024]{1,0:T(8,128)(2,1)}, u32[]{:S(2)}, u32[]{:S(2)}) %collective-permute-start.22) | collective-permute-done | bytes 1179680 | tf_op jit(solution)/shard_map/ppermute | solution.py:22
  215.2 8.5 %shard_map.132 = (bf16[2,288,768]{2,1,0:T(8,128)(2,1)S(1)}, bf16[576,4096]{1,0:T(8,128)(2,1)}) custom-call(bf16[576,1024]{1,0:T(8,128)(2,1)S(1)} %copy-done.3, bf16[576,1024]{1,0:T(8,128)(2,1)S(1)} %copy-done.5, bf16[576,1024]{1,0:T(8,128)(2,1)} %collective-permute-done.22.args_2_, bf16[576,1024]{1,0:T(8,128)(2,1)} %collective-permute-done.24.args_3_, ...), custom_call_target="tpu_custom_call" | custom-call | flops 3623878656 | bytes 15728640 | tf_op jit(solution)/shard_map/pallas_call | solution.py:310
  223.8 2.7 fusion.7
  226.6 7.4 %shard_map.133 = bf16[2,288,768]{2,1,0:T(8,128)(2,1)S(1)} custom-call(bf16[576,4096]{1,0:T(8,128)(2,1)} %get-tuple-element.36.hid.args_1_, bf16[4096,1536]{1,0:T(8,128)(2,1)} %bitcast.99, f32[576,128]{1,0:T(8,128)S(1)} %shard_map.131.args_5_.prob.args_2_.args_3_), custom_call_target="tpu_custom_call" | custom-call | flops 3623878656 | bytes 11010048 | tf_op jit(solution)/shard_map/pallas_call | solution.py:332
  235.7 2.0 collective-permute-start.27
  238.6 4.1 %all-to-all-start.2 = ((bf16[4,72,768]{2,1,0:T(8,128)(2,1)}), bf16[4,72,768]{2,1,0:T(8,128)(2,1)}, u32[]{:S(2)}, u32[]{:S(2)}) async-start(bf16[4,72,768]{2,1,0:T(8,128)(2,1)} %bitcast.38), calls=%async_computation.2 | async-start | bytes 884736 | tf_op jit(solution)/shard_map/all_to_all | solution.py:687
  243.9 4.4 %collective-permute-done.27 = bf16[288,768]{1,0:T(8,128)(2,1)} collective-permute-done((bf16[288,768]{1,0:T(8,128)(2,1)}, bf16[288,768]{1,0:T(8,128)(2,1)}, u32[]{:S(2)}, u32[]{:S(2)}) %collective-permute-start.27) | collective-permute-done | bytes 442400 | tf_op jit(solution)/shard_map/ppermute | solution.py:22
  248.2 2.0 fusion.15
  250.2 5.3 %all-to-all-done.2 = bf16[4,72,768]{2,1,0:T(8,128)(2,1)} async-done(((bf16[4,72,768]{2,1,0:T(8,128)(2,1)}), bf16[4,72,768]{2,1,0:T(8,128)(2,1)}, u32[]{:S(2)}, u32[]{:S(2)}) %all-to-all-start.2) | async-done | bytes 442400 | tf_op jit(solution)/shard_map/all_to_all | solution.py:687
  255.5 4.3 %all-to-all-start.3 = ((bf16[4,72,768]{2,1,0:T(8,128)(2,1)}), bf16[4,72,768]{2,1,0:T(8,128)(2,1)}, u32[]{:S(2)}, u32[]{:S(2)}) async-start(bf16[4,72,768]{2,1,0:T(8,128)(2,1)} %bitcast.106), calls=%async_computation.3 | async-start | bytes 884736 | tf_op jit(solution)/shard_map/all_to_all | solution.py:687
  259.9 14.5 %shard_map.136 = bf16[4096,1536]{1,0:T(8,128)(2,1)} custom-call(s32[1]{0:T(128)} %constant.139.clone.1.args_0_, bf16[576,4096]{1,0:T(8,128)(2,1)} %get-tuple-element.36.hid.args_1_, bf16[576,1664]{1,0:T(8,128)(2,1)S(1)} %bitcast.96, f32[576,128]{1,0:T(8,128)S(1)} %shard_map.131.args_5_.prob.args_2_.args_3_), custom_call_target="tpu_custom_call" | custom-call | flops 7247757312 | bytes 17301504 | tf_op jit(solution)/shard_map/pallas_call | solution.py:374
  274.3 2.8 fusion.3
  277.1 18.6 %shard_map.134 = bf16[6144,1024]{1,0:T(8,128)(2,1)} custom-call(bf16[576,6144]{1,0:T(8,128)(2,1)} %get-tuple-element.37.args_0_, bf16[576,1024]{1,0:T(8,128)(2,1)S(1)} %copy-done.2, f32[576,128]{1,0:T(8,128)S(1)} %shard_map.131.args_5_.prob.args_2_.args_3_, bf16[2,576,1024]{2,1,0:T(8,128)(2,1)} %get-tuple-element.30.args_3_, ...), custom_call_target="tpu_custom_call" | custom-call | flops 7247757312 | bytes 24379392 | tf_op jit(solution)/shard_map/pallas_call | solution.py:234
  295.7 18.5 %shard_map.135 = bf16[6144,1024]{1,0:T(8,128)(2,1)} custom-call(bf16[576,6144]{1,0:T(8,128)(2,1)} %get-tuple-element.37.args_0_, bf16[576,1024]{1,0:T(8,128)(2,1)S(1)} %copy-done.1, f32[576,128]{1,0:T(8,128)S(1)} %shard_map.131.args_5_.prob.args_2_.args_3_, bf16[2,576,1024]{2,1,0:T(8,128)(2,1)} %get-tuple-element.30.args_3_, ...), custom_call_target="tpu_custom_call" | custom-call | flops 7247757312 | bytes 24379392 | tf_op jit(solution)/shard_map/pallas_call | solution.py:234
  (139 shorter events, 46.5 us)
Async XLA Ops:
  0.6 17.8 %collective-permute-start.2 = (bf16[128,1536]{1,0:T(8,128)(2,1)}, bf16[128,1536]{1,0:T(8,128)(2,1)}, u32[]{:S(2)}, u32[]{:S(2)}) collective-permute-start(bf16[128,1536]{1,0:T(8,128)(2,1)} %param.10), channel_id=1, source_target_pairs={{0,2},{2,4},{4,6},{6,0},{1,3},{3,5},{5,7},{7,1},{8,10},{10,12},{12... | collective-permute-start | bytes 1179656 | tf_op jit(solution)/shard_map/ppermute | solution.py:22
  3.7 29.3 %collective-permute-start.3 = (bf16[128,1536]{1,0:T(8,128)(2,1)}, bf16[128,1536]{1,0:T(8,128)(2,1)}, u32[]{:S(2)}, u32[]{:S(2)}) collective-permute-start(bf16[128,1536]{1,0:T(8,128)(2,1)} %param.10), channel_id=1, source_target_pairs={{0,4},{2,6},{4,0},{6,2},{1,5},{3,7},{5,1},{7,3},{8,12},{10,14},{12... | collective-permute-start | bytes 1179656 | tf_op jit(solution)/shard_map/ppermute | solution.py:22
  6.3 27.8 %collective-permute-start.4 = (bf16[128,1536]{1,0:T(8,128)(2,1)}, bf16[128,1536]{1,0:T(8,128)(2,1)S(1)}, u32[]{:S(2)}, u32[]{:S(2)}) collective-permute-start(bf16[128,1536]{1,0:T(8,128)(2,1)} %param.10), channel_id=1, source_target_pairs={{0,6},{2,0},{4,2},{6,4},{1,7},{3,1},{5,3},{7,5},{8,14},{10,8},{12,... | collective-permute-start | bytes 1179656 | tf_op jit(solution)/shard_map/ppermute | solution.py:22
  7.7 52.5 %collective-permute-start.5 = (bf16[1536,768]{1,0:T(8,128)(2,1)}, bf16[1536,768]{1,0:T(8,128)(2,1)}, u32[]{:S(2)}, u32[]{:S(2)}) collective-permute-start(bf16[1536,768]{1,0:T(8,128)(2,1)} %param.11), channel_id=1, source_target_pairs={{0,1},{1,0},{2,3},{3,2},{4,5},{5,4},{6,7},{7,6},{8,9},{9,8},{10,11... | collective-permute-start | bytes 7077896 | tf_op jit(solution)/shard_map/ppermute | solution.py:22
  10.6 2.5 collective-permute-start.8
  13.1 5.2 %collective-permute-start.9 = (f32[5,3072]{1,0:T(8,128)S(1)}, f32[5,3072]{1,0:T(8,128)S(1)}, u32[]{:S(2)}, u32[]{:S(2)}) collective-permute-start(f32[5,3072]{1,0:T(8,128)S(1)} %pad_maximum_fusion.3), channel_id=1, source_target_pairs={{0,16},{16,0},{1,17},{17,1},{2,18},{18,2},{3,19},{19,3},{4,20},{20... | collective-permute-start | bytes 184328 | tf_op jit(solution)/shard_map/ppermute | solution.py:22
  18.4 46.2 %collective-permute-start.1 = (bf16[128,896]{1,0:T(8,128)(2,1)}, bf16[128,896]{1,0:T(8,128)(2,1)S(1)}, u32[]{:S(2)}, u32[]{:S(2)}) collective-permute-start(bf16[128,896]{1,0:T(8,128)(2,1)} %get-tuple-element.70), channel_id=1, source_target_pairs={{0,8},{1,9},{2,0},{3,1},{4,24},{5,25},{6,16},{7,17},{8,10},{9,11},... | collective-permute-start | bytes 688136 | tf_op jit(solution)/shard_map/ppermute | solution.py:568
  18.5 46.1 %collective-permute-start = (bf16[128,896]{1,0:T(8,128)(2,1)}, bf16[128,896]{1,0:T(8,128)(2,1)S(1)}, u32[]{:S(2)}, u32[]{:S(2)}) collective-permute-start(bf16[128,896]{1,0:T(8,128)(2,1)} %get-tuple-element.71), channel_id=1, source_target_pairs={{0,0},{1,1},{2,8},{3,9},{4,16},{5,17},{6,24},{7,25},{8,2},{9,3},{1... | collective-permute-start | bytes 688136 | tf_op jit(solution)/shard_map/ppermute | solution.py:568
  64.6 2.5 collective-permute-start.6
  67.5 11.5 %collective-permute-start.7 = (bf16[256,768]{1,0:T(8,128)(2,1)S(1)}, bf16[256,768]{1,0:T(8,128)(2,1)S(1)}, u32[]{:S(2)}, u32[]{:S(2)}) collective-permute-start(bf16[256,768]{1,0:T(8,128)(2,1)S(1)} %fusion.25), channel_id=1, source_target_pairs={{0,16},{16,0},{1,17},{17,1},{2,18},{18,2},{3,19},{19,3},{4,20},{20... | collective-permute-start | bytes 1179656 | tf_op jit(solution)/shard_map/ppermute | solution.py:22
  80.6 26.5 %all-to-all-start = ((bf16[4,144,768]{2,1,0:T(8,128)(2,1)}), bf16[4,144,768]{2,1,0:T(8,128)(2,1)S(1)}, u32[]{:S(2)}, u32[]{:S(2)}) async-start(bf16[4,144,768]{2,1,0:T(8,128)(2,1)} %bitcast.16), calls=%async_computation | async-start | bytes 1769472 | tf_op jit(solution)/shard_map/all_to_all | solution.py:614
  107.1 30.7 %collective-permute-start.13 = (bf16[4,144,768]{2,1,0:T(8,128)(2,1)S(1)}, bf16[4,144,768]{2,1,0:T(8,128)(2,1)S(1)}, u32[]{:S(2)}, u32[]{:S(2)}) collective-permute-start(bf16[4,144,768]{2,1,0:T(8,128)(2,1)S(1)} %all-to-all-done.args_0_), channel_id=1, source_target_pairs={{0,1},{1,0},{2,3},{3,2},{4,5},{5,4},{6,7},{7,6},{8,9},{9,8},{10,11... | collective-permute-start | bytes 2654216 | tf_op jit(solution)/shard_map/ppermute | solution.py:22
  107.1 28.0 %collective-permute-start.15 = (bf16[4,144,768]{2,1,0:T(8,128)(2,1)S(1)}, bf16[4,144,768]{2,1,0:T(8,128)(2,1)}, u32[]{:S(2)}, u32[]{:S(2)}) collective-permute-start(bf16[4,144,768]{2,1,0:T(8,128)(2,1)S(1)} %all-to-all-done.args_0_), channel_id=1, source_target_pairs={{0,16},{16,0},{1,17},{17,1},{2,18},{18,2},{3,19},{19,3},{4,20},{20... | collective-permute-start | bytes 2654216 | tf_op jit(solution)/shard_map/ppermute | solution.py:22
  110.8 30.5 %collective-permute-start.10 = (bf16[128,768]{1,0:T(8,128)(2,1)}, bf16[128,768]{1,0:T(8,128)(2,1)}, u32[]{:S(2)}, u32[]{:S(2)}) collective-permute-start(bf16[128,768]{1,0:T(8,128)(2,1)} %get-tuple-element.59), channel_id=1, source_target_pairs={{0,0},{1,1},{8,2},{9,3},{16,4},{17,5},{24,6},{25,7},{2,8},{3,9},{1... | collective-permute-start | bytes 589832 | tf_op jit(solution)/shard_map/ppermute | solution.py:621
  113.8 27.6 %collective-permute-start.11 = (bf16[128,768]{1,0:T(8,128)(2,1)}, bf16[128,768]{1,0:T(8,128)(2,1)}, u32[]{:S(2)}, u32[]{:S(2)}) collective-permute-start(bf16[128,768]{1,0:T(8,128)(2,1)} %get-tuple-element.60), channel_id=1, source_target_pairs={{8,0},{9,1},{0,2},{1,3},{24,4},{25,5},{16,6},{17,7},{10,8},{11,9},... | collective-permute-start | bytes 589832 | tf_op jit(solution)/shard_map/ppermute | solution.py:621
  113.8 37.8 %all-to-all-start.1 = ((bf16[4,72,1664]{2,1,0:T(8,128)(2,1)}), bf16[4,72,1664]{2,1,0:T(8,128)(2,1)}, u32[]{:S(2)}, u32[]{:S(2)}) async-start(bf16[4,72,1664]{2,1,0:T(8,128)(2,1)} %bitcast.29), calls=%async_computation.1 | async-start | bytes 1916928 | tf_op jit(solution)/shard_map/all_to_all | solution.py:638
  118.3 35.4 %collective-permute-start.12 = (bf16[4,144,768]{2,1,0:T(8,128)(2,1)S(1)}, bf16[4,144,768]{2,1,0:T(8,128)(2,1)S(1)}, u32[]{:S(2)}, u32[]{:S(2)}) collective-permute-start(bf16[4,144,768]{2,1,0:T(8,128)(2,1)S(1)} %all-to-all-done.args_0_), channel_id=1, source_target_pairs={{0,8},{8,0},{1,9},{9,1},{2,10},{10,2},{3,11},{11,3},{4,12},{12,4},... | collective-permute-start | bytes 2654216 | tf_op jit(solution)/shard_map/ppermute | solution.py:22
  136.1 10.4 %collective-permute-start.17 = (bf16[2,144,768]{2,1,0:T(8,128)(2,1)S(1)}, bf16[2,144,768]{2,1,0:T(8,128)(2,1)S(1)}, u32[]{:S(2)}, u32[]{:S(2)}) collective-permute-start(bf16[2,144,768]{2,1,0:T(8,128)(2,1)S(1)} %slice.82), channel_id=1, source_target_pairs={{0,1},{1,0},{2,3},{3,2},{4,5},{5,4},{6,7},{7,6},{8,9},{9,8},{10,11... | collective-permute-start | bytes 1327112 | tf_op jit(solution)/shard_map/ppermute | solution.py:22
  138.7 10.7 %collective-permute-start.19 = (bf16[2,144,768]{2,1,0:T(8,128)(2,1)S(1)}, bf16[2,144,768]{2,1,0:T(8,128)(2,1)S(1)}, u32[]{:S(2)}, u32[]{:S(2)}) collective-permute-start(bf16[2,144,768]{2,1,0:T(8,128)(2,1)S(1)} %slice.83), channel_id=1, source_target_pairs={{0,16},{16,0},{1,17},{17,1},{2,18},{18,2},{3,19},{19,3},{4,20},{20... | collective-permute-start | bytes 1327112 | tf_op jit(solution)/shard_map/ppermute | solution.py:22
  141.3 12.3 %collective-permute-start.14 = (bf16[4,144,768]{2,1,0:T(8,128)(2,1)}, bf16[4,144,768]{2,1,0:T(8,128)(2,1)}, u32[]{:S(2)}, u32[]{:S(2)}) collective-permute-start(bf16[4,144,768]{2,1,0:T(8,128)(2,1)} %copy-done.11), channel_id=1, source_target_pairs={{0,8},{8,0},{1,9},{9,1},{2,10},{10,2},{3,11},{11,3},{4,12},{12,4},... | collective-permute-start | bytes 2654216 | tf_op jit(solution)/shard_map/ppermute | solution.py:22
  141.4 12.3 %collective-permute-start.16 = (bf16[4,144,768]{2,1,0:T(8,128)(2,1)}, bf16[4,144,768]{2,1,0:T(8,128)(2,1)}, u32[]{:S(2)}, u32[]{:S(2)}) collective-permute-start(bf16[4,144,768]{2,1,0:T(8,128)(2,1)} %collective-permute-done.15.args_4_), channel_id=1, source_target_pairs={{0,8},{8,0},{1,9},{9,1},{2,10},{10,2},{3,11},{11,3},{4,12},{12,4},... | collective-permute-start | bytes 2654216 | tf_op jit(solution)/shard_map/ppermute | solution.py:22
  146.5 7.2 %collective-permute-start.18 = (bf16[2,144,768]{2,1,0:T(8,128)(2,1)S(1)}, bf16[2,144,768]{2,1,0:T(8,128)(2,1)S(1)}, u32[]{:S(2)}, u32[]{:S(2)}) collective-permute-start(bf16[2,144,768]{2,1,0:T(8,128)(2,1)S(1)} %collective-permute-done.17.args_6_), channel_id=1, source_target_pairs={{0,8},{8,0},{1,9},{9,1},{2,10},{10,2},{3,11},{11,3},{4,12},{12,4},... | collective-permute-start | bytes 1327112 | tf_op jit(solution)/shard_map/ppermute | solution.py:22
  151.6 33.0 %collective-permute-start.23 = (bf16[4,72,1664]{2,1,0:T(8,128)(2,1)}, bf16[4,72,1664]{2,1,0:T(8,128)(2,1)}, u32[]{:S(2)}, u32[]{:S(2)}) collective-permute-start(bf16[4,72,1664]{2,1,0:T(8,128)(2,1)} %all-to-all-done.1), channel_id=1, source_target_pairs={{0,1},{1,0},{2,3},{3,2},{4,5},{5,4},{6,7},{7,6},{8,9},{9,8},{10,11... | collective-permute-start | bytes 2875400 | tf_op jit(solution)/shard_map/ppermute | solution.py:22
  183.2 3.2 %collective-permute-start.21 = (bf16[576,1024]{1,0:T(8,128)(2,1)}, bf16[576,1024]{1,0:T(8,128)(2,1)S(1)}, u32[]{:S(2)}, u32[]{:S(2)}) collective-permute-start(bf16[576,1024]{1,0:T(8,128)(2,1)} %get-tuple-element.26.args_0_), channel_id=1, source_target_pairs={{0,8},{8,0},{1,9},{9,1},{2,10},{10,2},{3,11},{11,3},{4,12},{12,4},... | collective-permute-start | bytes 3538952 | tf_op jit(solution)/shard_map/ppermute | solution.py:22
  183.3 28.7 %collective-permute-start.22 = (bf16[576,1024]{1,0:T(8,128)(2,1)}, bf16[576,1024]{1,0:T(8,128)(2,1)}, u32[]{:S(2)}, u32[]{:S(2)}) collective-permute-start(bf16[576,1024]{1,0:T(8,128)(2,1)} %get-tuple-element.26.args_0_), channel_id=1, source_target_pairs={{0,16},{16,0},{1,17},{17,1},{2,18},{18,2},{3,19},{19,3},{4,20},{20... | collective-permute-start | bytes 3538952 | tf_op jit(solution)/shard_map/ppermute | solution.py:22
  201.4 22.4 %collective-permute-start.26 = (bf16[2,576,1024]{2,1,0:T(8,128)(2,1)}, bf16[2,576,1024]{2,1,0:T(8,128)(2,1)}, u32[]{:S(2)}, u32[]{:S(2)}) collective-permute-start(bf16[2,576,1024]{2,1,0:T(8,128)(2,1)} %get-tuple-element.35), channel_id=1, source_target_pairs={{0,8},{8,0},{1,9},{9,1},{2,10},{10,2},{3,11},{11,3},{4,12},{12,4},... | collective-permute-start | bytes 7077896 | tf_op jit(solution)/shard_map/ppermute | solution.py:22
  212.0 3.2 %collective-permute-start.24 = (bf16[576,1024]{1,0:T(8,128)(2,1)}, bf16[576,1024]{1,0:T(8,128)(2,1)}, u32[]{:S(2)}, u32[]{:S(2)}) collective-permute-start(bf16[576,1024]{1,0:T(8,128)(2,1)} %collective-permute-done.22.args_2_), channel_id=1, source_target_pairs={{0,8},{8,0},{1,9},{9,1},{2,10},{10,2},{3,11},{11,3},{4,12},{12,4},... | collective-permute-start | bytes 3538952 | tf_op jit(solution)/shard_map/ppermute | solution.py:22
  223.7 14.0 %collective-permute-start.25 = (bf16[288,768]{1,0:T(8,128)(2,1)S(1)}, bf16[288,768]{1,0:T(8,128)(2,1)S(1)}, u32[]{:S(2)}, u32[]{:S(2)}) collective-permute-start(bf16[288,768]{1,0:T(8,128)(2,1)S(1)} %dynamic-slice_bitcast_fusion.1), channel_id=1, source_target_pairs={{0,1},{1,0},{2,3},{3,2},{4,5},{5,4},{6,7},{7,6},{8,9},{9,8},{10,11... | collective-permute-start | bytes 1327112 | tf_op jit(solution)/shard_map/ppermute | solution.py:22
  235.7 12.5 %collective-permute-start.27 = (bf16[288,768]{1,0:T(8,128)(2,1)}, bf16[288,768]{1,0:T(8,128)(2,1)}, u32[]{:S(2)}, u32[]{:S(2)}) collective-permute-start(bf16[288,768]{1,0:T(8,128)(2,1)} %dynamic-slice_bitcast_fusion), channel_id=1, source_target_pairs={{0,1},{1,0},{2,3},{3,2},{4,5},{5,4},{6,7},{7,6},{8,9},{9,8},{10,11... | collective-permute-start | bytes 1327112 | tf_op jit(solution)/shard_map/ppermute | solution.py:22
  238.6 16.9 %all-to-all-start.2 = ((bf16[4,72,768]{2,1,0:T(8,128)(2,1)}), bf16[4,72,768]{2,1,0:T(8,128)(2,1)}, u32[]{:S(2)}, u32[]{:S(2)}) async-start(bf16[4,72,768]{2,1,0:T(8,128)(2,1)} %bitcast.38), calls=%async_computation.2 | async-start | bytes 884736 | tf_op jit(solution)/shard_map/all_to_all | solution.py:687
  242.7 34.4 %collective-permute-start.28 = (bf16[576,1024]{1,0:T(8,128)(2,1)}, bf16[576,1024]{1,0:T(8,128)(2,1)S(1)}, u32[]{:S(2)}, u32[]{:S(2)}) collective-permute-start(bf16[576,1024]{1,0:T(8,128)(2,1)} %fusion.7), channel_id=1, source_target_pairs={{0,16},{16,0},{1,17},{17,1},{2,18},{18,2},{3,19},{19,3},{4,20},{20... | collective-permute-start | bytes 3538952 | tf_op jit(solution)/shard_map/ppermute | solution.py:22
  255.5 18.8 %all-to-all-start.3 = ((bf16[4,72,768]{2,1,0:T(8,128)(2,1)}), bf16[4,72,768]{2,1,0:T(8,128)(2,1)}, u32[]{:S(2)}, u32[]{:S(2)}) async-start(bf16[4,72,768]{2,1,0:T(8,128)(2,1)} %bitcast.106), calls=%async_computation.3 | async-start | bytes 884736 | tf_op jit(solution)/shard_map/all_to_all | solution.py:687
  (16 other events, 114.4 us)
